TPU v7x, 32 devices: a whole 2x2x4 slice. The times are simulated.
32 devices in a mesh: tm: 4 (over x, core), ctx: 8 (over z, y).
Axes of the slice: x: 2, y: 2, z: 4, core: 2. Of those that a mesh axis runs over, the one named last changes fastest.
Arguments:
- iterate: float32 [4, 1344, 1536], P('tm', 'ctx'), may hold values from -6 to 6
- anchor: float32 [1344, 1536], P('ctx'), may hold values from -6 to 6
- frame_index: int32 [1344], P('ctx'), may hold values from 0 to 7, never falling along the last dimension, each value on 1 to 336 neighbouring positions
- noise_steps: int32 [4, 8], P('tm'), may hold values from 0 to 11
- qkv_weight: bfloat16 [1536, 4608], replicated, may hold values from -0.15625 to 0.15625
- out_weight: bfloat16 [1536, 1536], replicated, may hold values from -0.15625 to 0.15625
- mod_weight: bfloat16 [256, 4608], replicated, may hold values from -0.375 to 0.375
Outputs:
- updated: float32 [4, 1344, 1536], P('tm', 'ctx')
Inputs may be any that keep to these rules, and one draw needn't show every extreme that they name: `frame_index`: frame numbers never fall along the sequence; each of the 8 frames holds 1 to 336 tokens.
All inputs are finite; a program needn't handle non-finite values.
Results may differ from a plain program's by a relative error of at most 0.00051.
Values may be sent and summed in bfloat16 or wider, within the bound.
A program may use at most 192 MiB of HBM per device.

v0:
```python
import math

import jax
import jax.numpy as jnp
from jax import lax
from jax.sharding import PartitionSpec as P

HD = 128
NSCHED = 12


shift_factor = 5.0
norm_eps = 1e-06


def carried_in(part, axis, combine, identity):
    place = lax.axis_index(axis)
    gathered = lax.all_gather(part, axis)
    state = jnp.zeros_like(part) + jnp.asarray(identity, part.dtype)

    def one(turn, state):
        return combine(state, lax.dynamic_index_in_dim(gathered, turn, 0, False))

    return lax.fori_loop(0, place, one, state)


def noise_level(level_index):
    fraction = level_index / NSCHED
    return shift_factor * fraction / (1.0 + (shift_factor - 1.0) * fraction)


def frame_terms(steps_row, mod_weight):
    level_float = steps_row.astype(jnp.float32)
    upper = noise_level(level_float + 1.0)
    lower = noise_level(level_float)
    step_size = upper - lower
    half_freq = mod_weight.shape[0] // 2
    rates = jnp.exp(-math.log(10000.0) * jnp.arange(half_freq, dtype=jnp.float32) / half_freq)
    angles = (1000.0 * upper)[:, None] * rates[None, :]
    features = jnp.concatenate([jnp.cos(angles), jnp.sin(angles)], axis=1).astype(jnp.bfloat16)
    modulation = jnp.dot(features, mod_weight, preferred_element_type=jnp.float32)
    return (modulation, step_size)


def layer_norm(latent):
    center = latent - jnp.mean(latent, axis=-1, keepdims=True)
    spread = jnp.mean(center * center, axis=-1, keepdims=True)
    return center * lax.rsqrt(spread + norm_eps)


def head_norm(projected):
    tok_rows = projected.shape[0]
    model_width = projected.shape[1]
    split = projected.reshape(tok_rows, model_width // HD, HD)
    scaled = split * lax.rsqrt(jnp.mean(split * split, axis=-1, keepdims=True) + norm_eps)
    return scaled.reshape(tok_rows, model_width).astype(jnp.bfloat16)


def attend(query_heads, key_rows, value_rows, frame_piece, frame_index):
    piece_rows = key_rows.shape[0]
    head_count = query_heads.shape[1]
    key_heads = key_rows.reshape(piece_rows, head_count, HD)
    value_heads = value_rows.reshape(piece_rows, head_count, HD)
    scores = jnp.einsum(
        "qhd,khd->hqk", query_heads, key_heads, preferred_element_type=jnp.float32
    ) * HD ** (-0.5)
    allowed = frame_piece[None, :] <= frame_index[:, None]
    weights = jnp.where(allowed[None, :, :], jnp.exp(scores), 0.0)
    numerator = jnp.einsum(
        "hqk,khd->hqd",
        weights.astype(jnp.bfloat16),
        value_heads,
        preferred_element_type=jnp.float32,
    )
    denominator = jnp.sum(weights, axis=-1)
    return (numerator, denominator)


def velocity_drift(latent, steps_row, frame_index, qkv_weight, out_weight, mod_weight):
    tok_rows = latent.shape[0]
    model_width = latent.shape[1]
    head_count = model_width // HD
    frame_count = steps_row.shape[0]
    modulation, step_size = frame_terms(steps_row, mod_weight)
    one_hot = (frame_index[:, None] == jnp.arange(frame_count, dtype=jnp.int32)[None, :]).astype(
        jnp.float32
    )
    tok_mod = jnp.dot(one_hot, modulation, precision=lax.Precision.HIGHEST)
    tok_step = jnp.dot(one_hot, step_size[:, None], precision=lax.Precision.HIGHEST)[:, 0]
    shift_part = tok_mod[:, :model_width]
    scale_part = tok_mod[:, model_width : 2 * model_width]
    gate_part = tok_mod[:, 2 * model_width :]
    normed = (layer_norm(latent) * (1.0 + scale_part) + shift_part).astype(jnp.bfloat16)
    queries = head_norm(
        jnp.dot(normed, qkv_weight[:, :model_width], preferred_element_type=jnp.float32)
    )
    query_heads = queries.reshape(tok_rows, head_count, HD)
    kv_weight = qkv_weight[:, model_width:]
    kv_rows = jnp.dot(
        lax.all_gather(normed, "ctx", axis=0, tiled=True),
        kv_weight,
        preferred_element_type=jnp.float32,
    )
    key_rows = head_norm(kv_rows[:, :model_width])
    values = kv_rows[:, model_width:].astype(jnp.bfloat16)
    numerator, denominator = attend(
        query_heads,
        key_rows,
        values,
        lax.all_gather(frame_index, "ctx", axis=0, tiled=True),
        frame_index,
    )
    attended = (numerator / denominator[:, :, None]).astype(jnp.bfloat16)
    attended = attended.transpose(1, 0, 2).reshape(tok_rows, model_width)
    branch = jnp.dot(attended, out_weight, preferred_element_type=jnp.float32)
    return -tok_step[:, None] * (latent + gate_part * branch)


def add_terms(earlier, later):
    return earlier + later


def per_device(iterate, anchor, frame_index, noise_steps, qkv_weight, out_weight, mod_weight):
    position = 0
    drifts = [
        velocity_drift(
            iterate[position],
            noise_steps[position],
            frame_index,
            qkv_weight,
            out_weight,
            mod_weight,
        )
    ]
    block_total = drifts[0]
    earlier = carried_in(block_total, "tm", add_terms, jnp.zeros_like(block_total))
    running = earlier
    position = 0
    running = running + drifts[position]
    results = [anchor + running]
    return jnp.stack(results, axis=0)


def solution(mesh):
    placed = (P("tm", "ctx", None), P("ctx", None), P("ctx"), P("tm", None), P(), P(), P())
    return jax.shard_map(
        per_device, mesh=mesh, in_specs=placed, out_specs=P("tm", "ctx", None), check_vma=False
    )
```

profile of v0, /device:TPU:3, one launch (start us, length us, event | category | flops | bytes accessed | tf_op | source)
XLA Modules:
  0.0 234.4 jit_solution(15650006352869661818)
XLA Ops:
  6.6 0.8 multiply_bitcast_fusion
  7.4 1.6 reduce_sum.45
  8.9 1.5 multiply_reduce_fusion
  10.4 0.1 fusion.34
  10.5 0.4 fusion.36
  10.9 2.1 fusion.30
  13.1 1.6 copy-done.4
  14.7 1.1 fusion.17
  15.8 0.0 all-gather.4.cloned.1.call-update
  15.8 0.0 all-gather.6.cloned.1.call-start
  15.9 0.0 copy-start.5
  15.9 0.0 copy-start.6
  15.9 0.0 copy-start.7
  15.9 4.8 %fusion.54 = (f32[168,1536]{1,0:T(8,128)}, f32[168,1536]{1,0:T(8,128)}) fusion(bf16[168,1536]{1,0:T(8,128)(2,1)} %fusion.17, bf16[1536,4608]{1,0:T(8,128)(2,1)} %param.13), kind=kOutput, calls=%fused_computation.72 | convolution fusion | flops 792981504 | bytes 7299072 | tf_op jit(solution)/shard_map/dot_general | solution.py:95
  20.7 1.4 mul.143
  22.1 0.4 reduce_sum.47
  22.5 0.1 copy.28
  22.6 0.1 copy.29
  22.8 0.2 fusion.31
  23.0 0.0 copy-done.7
  23.0 0.6 dynamic-slice
  24.3 0.3 dynamic-update-slice
  24.6 11.0 %all-reduce = s32[1344]{0:T(1024)S(1)} all-reduce(s32[1344]{0:T(1024)S(1)} %dynamic-update-slice), channel_id=1, replica_groups=mesh['tm'=4,'ctx'=8] {'ctx'}, use_global_device_ids=true, to_apply=%add | all-reduce | flops 1344 | bytes 10752
  35.6 0.2 broadcast_compare_fusion
  35.8 53.1 %all-gather.4.cloned.1.call-done = bf16[1344,1536]{1,0:T(8,128)(2,1)} async-done(((bf16[168,1536]{1,0:T(8,128)(2,1)}), bf16[1344,1536]{1,0:T(8,128)(2,1)}) %all-gather.4.cloned.1.call-update) | async-done | bytes 4128784 | tf_op jit(solution)/shard_map/all_gather | solution.py:100
  88.9 17.1 %fusion = f32[1344,3072]{1,0:T(8,128)S(1)} fusion(bf16[1344,1536]{1,0:T(8,128)(2,1)} %all-gather.4.cloned.1.call-done, bf16[1536,4608]{1,0:T(8,128)(2,1)} %param.13), kind=kOutput, calls=%fused_computation.2 | convolution fusion | flops 12683575296 | bytes 30081024 | tf_op jit(solution)/shard_map/dot_general | solution.py:99
  106.1 4.6 %slice_multiply_fusion = f32[1344,1536]{1,0:T(8,128)} fusion(f32[1344,3072]{1,0:T(8,128)S(1)} %fusion), kind=kLoop, calls=%fused_computation.8 | loop fusion | flops 2064384 | bytes 16515072 | tf_op jit(solution)/shard_map/mul | solution.py:55
  110.7 3.5 %copy-done.2 = f32[1344,3072]{1,0:T(8,128)} copy-done((f32[1344,3072]{1,0:T(8,128)}, f32[1344,3072]{1,0:T(8,128)S(1)}, u32[]{:S(2)}) %copy-start.2) | copy-done | bytes 16515096
  114.2 2.6 %slice.50 = bf16[1344,1536]{1,0:T(8,128)(2,1)} slice(f32[1344,3072]{1,0:T(8,128)S(1)} %fusion), slice={[0:1344], [1536:3072]} | slice | bytes 8257536 | tf_op jit(solution)/shard_map/slice | solution.py:105
  116.8 9.0 %copy.30 = f32[1344,1536]{0,1:T(8,128)} copy(f32[1344,1536]{1,0:T(8,128)} %slice_multiply_fusion) | data formatting | bytes 16515072 | tf_op jit(solution)/shard_map/mul | solution.py:55
  125.8 4.0 %reduce_sum.48 = f32[1344,12]{0,1:T(8,128)S(1)} reduce(f32[1344,12,128]{0,2,1:T(8,128)} %bitcast.63, f32[]{:T(128)} %constant.20.clone.1), dimensions={2}, to_apply=%region_3.0 | reduce | flops 2048256 | bytes 8322052 | tf_op jit(solution)/shard_map/reduce_sum | solution.py:55
  129.8 3.8 %mul.149 = f32[1344,12,128]{0,2,1:T(8,128)} broadcast(f32[1344,12]{0,1:T(8,128)S(1)} %add_rsqrt_fusion), dimensions={0,1} | broadcast | bytes 8322048 | tf_op jit(solution)/shard_map/mul | solution.py:55
  133.7 9.0 %copy.31 = f32[1344,1536]{1,0:T(8,128)} copy(f32[1344,1536]{0,1:T(8,128)} %bitcast.64) | data formatting | bytes 16515072 | tf_op jit(solution)/shard_map/mul | solution.py:55
  142.6 9.0 %multiply_convert_fusion = bf16[1344,1536]{1,0:T(8,128)(2,1)} fusion(f32[1344,1536]{1,0:T(8,128)} %copy.31, f32[1344,3072]{1,0:T(8,128)} %copy-done.2), kind=kLoop, calls=%fused_computation.7 | loop fusion | flops 4128768 | bytes 20643840 | tf_op jit(solution)/shard_map/convert_element_type | solution.py:56
  151.6 6.5 %copy.32 = bf16[1344,1536]{0,1:T(8,128)(2,1)} copy(bf16[1344,1536]{1,0:T(8,128)(2,1)} %multiply_convert_fusion) | data formatting | bytes 8257536 | tf_op jit(solution)/shard_map/convert_element_type | solution.py:56
  158.1 6.4 %copy.35 = bf16[1344,1536]{0,1:T(8,128)(2,1)} copy(bf16[1344,1536]{1,0:T(8,128)(2,1)} %slice.50) | data formatting | bytes 8257536 | tf_op jit(solution)/shard_map/slice | solution.py:105
  164.6 0.4 mul.144
  165.0 10.0 %fusion.2 = (f32[12,168]{1,0:T(8,128)S(1)}, f32[12,168,1344]{2,1,0:T(8,128)}) fusion(pred[168,1344]{1,0:T(8,128)(4,1)S(1)} %broadcast_compare_fusion, bf16[1344,12,128]{0,2,1:T(8,128)(2,1)} %bitcast.65, f32[168,1536]{1,0:T(8,128)} %get-tuple-element.42, f32[21,8,12,128]{3,2,1,0:T(8,128)S(1)} %bitcast.68), kind=kOutput, calls=%fused_computation.4 | convolution fusion | flops 702275584 | bytes 17265024 | tf_op jit(solution)/shard_map/qhd,khd->hqk/dot_general | solution.py:64
  175.0 7.5 %fusion.21 = bf16[12,21,8,128]{3,2,1,0:T(8,128)(2,1)S(1)} fusion(bf16[1344,12,128]{0,2,1:T(8,128)(2,1)} %bitcast.67, f32[12,168,1344]{2,1,0:T(8,128)} %get-tuple-element.44, pred[168,1344]{1,0:T(8,128)(4,1)S(1)} %broadcast_compare_fusion, f32[168,12]{0,1:T(8,128)S(1)} %bitcast.69), kind=kOutput, calls=%fused_computation.29 | convolution fusion | flops 702277632 | bytes 15716736 | tf_op jit(solution)/shard_map/hqk,khd->hqd/dot_general | solution.py:69
  182.5 4.6 %fusion.12 = f32[168,1536]{1,0:T(8,128)} fusion(bf16[1536,1536]{1,0:T(8,128)(2,1)} %param.14, f32[168,4608]{1,0:T(8,128)} %copy-done.4, f32[1,168,1536]{2,1,0:T(8,128)S(1)} %copy-done.3, bf16[12,21,8,128]{3,2,1,0:T(8,128)(2,1)S(1)} %fusion.21, f32[168]{0:T(256)S(1)} %neg.4), kind=kOutput, calls=%fused_computation.17 | convolution fusion | flops 793497600 | bytes 8331936 | tf_op jit(solution)/shard_map/dot_general | solution.py:115
  187.1 0.0 all-gather.6.cloned.1.call-update
  187.1 33.0 %all-gather.6.cloned.1.call-done = f32[672,1536]{1,0:T(8,128)} async-done(((f32[168,1536]{1,0:T(8,128)}), f32[672,1536]{1,0:T(8,128)}) %all-gather.6.cloned.1.call-update) | async-done | bytes 4128784 | tf_op jit(solution)/shard_map/all_gather | solution.py:18
  220.1 0.1 broadcast_in_dim.10
  220.2 4.5 %while.10 = (s32[]{:T(128)}, f32[168,1536]{1,0:T(8,128)S(1)}, s32[]{:T(128)}, f32[4,168,1536]{2,1,0:T(8,128)}, s32[]{:T(128)}, /*index=5*/s32[]{:T(128)}, s32[]{:T(128)}) while((s32[]{:T(128)}, f32[168,1536]{1,0:T(8,128)S(1)}, s32[]{:T(128)}, f32[4,168,1536]{2,1,0:T(8,128)}, s32[]{:T(128)}, /*index=5*/s32[]{:T(128)}, s32[]{:T(128)}) %tuple.29), condition=%wide.region_6.7_spmd, body=%wide.region_5.6_spmd.sunk | while | flops 258053 | bytes 3096691 | solution.py:24
  220.2 1.5 bitcast_add_fusion.2
  221.7 1.5 bitcast_add_fusion.2
  223.2 1.5 bitcast_add_fusion.2
  224.7 2.8 %add_bitcast_fusion = f32[1,168,1536]{2,1,0:T(8,128)} fusion(f32[168,1536]{1,0:T(8,128)} %param.10, f32[168,1536]{1,0:T(8,128)S(1)} %get-tuple-element.28, f32[168,1536]{1,0:T(8,128)} %fusion.12), kind=kLoop, calls=%fused_computation.26 | loop fusion | flops 516096 | bytes 4128768 | tf_op jit(solution)/shard_map/stack | solution.py:141
  (18 shorter events, 0.1 us)
Async XLA Ops:
  6.5 4.0 %copy-start = (bf16[256,4608]{1,0:T(8,128)(2,1)S(1)}, bf16[256,4608]{1,0:T(8,128)(2,1)}, u32[]{:S(2)}) copy-start(bf16[256,4608]{1,0:T(8,128)(2,1)} %param.15) | copy-start | bytes 7077892
  6.5 8.1 %copy-start.3 = (f32[1,168,1536]{2,1,0:T(8,128)S(1)}, f32[1,168,1536]{2,1,0:T(8,128)}, u32[]{:S(2)}) copy-start(f32[1,168,1536]{2,1,0:T(8,128)} %param.9) | copy-start | bytes 3096580
  6.5 82.4 %all-gather.4.cloned.1.call-start = ((), (), s32[]{:S(2)}) async-start(), calls=%async_computation | async-start | bytes 4644864 | tf_op jit(solution)/shard_map/all_gather | solution.py:100
  13.0 1.6 copy-start.4
  15.8 204.3 %all-gather.6.cloned.1.call-start = ((), (), s32[]{:S(2)}) async-start(), calls=%async_computation.1 | async-start | bytes 5160960 | tf_op jit(solution)/shard_map/all_gather | solution.py:18
  15.9 6.9 %copy-start.5 = (s32[168]{0:T(256)S(1)}, s32[168]{0:T(256)}, u32[]{:S(2)}) copy-start(s32[168]{0:T(256)} %param.11) | copy-start | bytes 2020
  15.9 6.9 %copy-start.6 = (s32[1,8]{1,0:T(1,128)S(1)}, s32[1,8]{1,0:T(1,128)}, u32[]{:S(2)}) copy-start(s32[1,8]{1,0:T(1,128)} %param.12) | copy-start | bytes 100
  15.9 7.1 %copy-start.7 = (u32[32]{0:T(128)S(1)}, u32[32]{0:T(128)}, u32[]{:S(2)}) copy-start(u32[32]{0:T(128)} %constant.58) | copy-start | bytes 388
  106.1 8.1 %copy-start.2 = (f32[1344,3072]{1,0:T(8,128)}, f32[1344,3072]{1,0:T(8,128)S(1)}, u32[]{:S(2)}) copy-start(f32[1344,3072]{1,0:T(8,128)S(1)} %fusion) | copy-start | bytes 49545220
  224.7 2.9 %copy-start.1 = (bf16[256,4608]{1,0:T(8,128)(2,1)S(1)}, bf16[256,4608]{1,0:T(8,128)(2,1)}, u32[]{:S(2)}) copy-start(bf16[256,4608]{1,0:T(8,128)(2,1)} %param.15) | copy-start | bytes 7077892
Sparse Core Ops, SparseCore 0:
  15.9 72.9 all-gather.3
  187.2 32.8 all-gather.5
where the time goes:
time: 236 us; the launch traced here: 234 us
  waiting for transfers between devices  86.1 us (36%)
  matrix products  46.7 us (20%)
  local copies, waits for them, and re-layouts  45.5 us (19%)
  other arithmetic  30.7 us (13%)
  between operations  14.3 us (6%)
  blocking collectives  11 us (5%)
    all_gather x1, waiting for transfers between devices, velocity_drift(): lax.all_gather(normed, 'ctx', axis=0, tiled=True)  53.1 us
    all_gather x1, waiting for transfers between devices, carried_in(): gathered = lax.all_gather(part, axis)  33 us
    dot_general x1, matrix products, velocity_drift(): jnp.dot(lax.all_gather(normed, 'ctx', axis=0, tiled=True), kv_weight, pre...  17.1 us
    mul x3, local copies, waits for them, and re-layouts, head_norm(): split * lax.rsqrt(jnp.mean(split * split, axis=-1, keepdims=True) + norm_...  13.2 us
    unnamed x1, blocking collectives  11 us
    mul x2, local copies, waits for them, and re-layouts, head_norm(): split * split  10.4 us
    dot_general x1, matrix products, attend(): jnp.einsum('qhd,khd->hqk', query_heads, key_heads, preferred_element_type...  10 us
    slice x2, local copies, waits for them, and re-layouts, velocity_drift(): values = kv_rows[:, model_width:].astype(jnp.bfloat16)  9.05 us
  transfers between devices with their start and end apart: 2, of which 2 were waited for; matrix products, arithmetic and copies ran while one was open for 3% of the time, Pallas kernels for 0%

commit v1 on v0

v1 whole, which is shorter than its diff:
```python
import functools
import math

import jax
import jax.numpy as jnp
from jax import lax
from jax.experimental import pallas as pl
from jax.experimental.pallas import tpu as pltpu
from jax.sharding import PartitionSpec as P

HD = 128
NSCHED = 12
MESH = pl.DeviceIdType.MESH

shift_factor = 5.0
norm_eps = 1e-06


def noise_level(level_index):
    fraction = level_index / NSCHED
    return shift_factor * fraction / (1.0 + (shift_factor - 1.0) * fraction)


def token_terms(steps_row, frame_index, freq):
    frame_count = steps_row.shape[0]
    hit = frame_index[:, None] == jnp.arange(frame_count, dtype=jnp.int32)[None, :]
    level_index = jnp.sum(jnp.where(hit, steps_row[None, :], 0), axis=1).astype(jnp.float32)
    upper = noise_level(level_index + 1.0)
    lower = noise_level(level_index)
    half_freq = freq // 2
    rates = jnp.exp(-math.log(10000.0) * jnp.arange(half_freq, dtype=jnp.float32) / half_freq)
    angles = (1000.0 * upper)[:, None] * rates[None, :]
    features = jnp.concatenate([jnp.cos(angles), jnp.sin(angles)], axis=1).astype(jnp.bfloat16)
    return features, (upper - lower)[:, None]


def kernel(
    tm_size, ctx_size,
    latent_ref, anchor_ref, feat_ref, gap_ref, frow_ref, qkv_ref, wo_ref, mod_ref,
    out_ref,
    wqkv, wo, wmod, own, buf, qbuf, acc, atts, attr, negate, drift, pdrift, xsend, xrecv, etot,
    w_sem, swap_send, swap_recv, ring_send, ring_recv, core_send, core_recv,
    att_send, att_recv, d_send, d_recv, x_send, x_recv, e_send, e_recv,
):
    R, D = latent_ref.shape[1], latent_ref.shape[2]
    half = D // 2
    Rp = own.shape[1]
    ring = ctx_size // 2
    pairs = tm_size // 2
    mid = ring // 2
    t = lax.axis_index("tm")
    c = lax.axis_index("ctx")
    a, k = t // 2, t % 2
    h, r = c // ring, c % ring
    u = r // 2
    p = 2 * u + (r % 2 + u) % 2

    def at_ring(q):
        v = q // 2
        return h * ring + 2 * v + (q % 2 + v) % 2

    core_peer = {"tm": 2 * a + 1 - k}
    swap_peer = {"tm": 2 * a + h, "ctx": k * ring + r}
    right = {"ctx": at_ring((p + 1) % ring)}
    left = {"ctx": at_ring((p + ring - 1) % ring)}

    loads = [pltpu.make_async_copy(mod_ref, wmod, w_sem.at[0])]
    for i in range(3):
        col = pl.multiple_of(i * D + k * half, 128)
        loads.append(pltpu.make_async_copy(qkv_ref.at[:, pl.ds(col, half)], wqkv.at[i], w_sem.at[1 + i]))
    loads.append(pltpu.make_async_copy(wo_ref, wo, w_sem.at[4]))
    for load in loads:
        load.start()

    barrier = pltpu.get_barrier_semaphore()
    greeted = [
        core_peer,
        {"tm": 2 * a + k, "ctx": (1 - h) * ring + r},
        {"tm": 2 * a + 1 - k, "ctx": (1 - h) * ring + r},
        left,
        right,
    ]
    for d in range(1, pairs):
        greeted.append({"tm": 2 * ((a + d) % pairs) + k})
    for peer in greeted:
        pl.semaphore_signal(barrier, inc=1, device_id=peer, device_id_type=MESH)

    x = latent_ref[0]
    center = x - jnp.mean(x, axis=-1, keepdims=True)
    spread = jnp.mean(center * center, axis=-1, keepdims=True)
    unit = center * lax.rsqrt(spread + norm_eps)
    loads[0].wait()
    feat = feat_ref[...]
    gap = gap_ref[...]
    for j in range(2):
        js = slice(j * half, (j + 1) * half)
        shift = jnp.dot(feat, wmod[:, j * half:(j + 1) * half], preferred_element_type=jnp.float32)
        scale = jnp.dot(feat, wmod[:, D + j * half:D + (j + 1) * half], preferred_element_type=jnp.float32)
        rows = unit[:, js] * (1.0 + scale) + shift
        tail = frow_ref[...] if j == 0 else jnp.zeros((Rp - R, half), jnp.float32)
        own[j] = jnp.concatenate([rows, tail], axis=0).astype(jnp.bfloat16)
    pl.semaphore_wait(barrier, len(greeted))

    def remote(src, dst, s_sem, r_sem, peer):
        return pltpu.make_async_remote_copy(
            src_ref=src, dst_ref=dst, send_sem=s_sem, recv_sem=r_sem, device_id=peer, device_id_type=MESH
        )

    def swap_copy(j):
        return remote(own.at[j], buf.at[0, j, h], swap_send.at[j], swap_recv.at[j], swap_peer)

    def swap_landed(j):
        return remote(own.at[j], buf.at[0, j, k], swap_send.at[j], swap_recv.at[j], swap_peer)

    @pl.when(k != h)
    def _():
        for j in range(2):
            swap_copy(j).start()

    @pl.when(k == h)
    def _():
        for j in range(2):
            buf[0, j, k] = own[j]

    @pl.when(k != h)
    def _():
        for j in range(2):
            swap_landed(j).wait_recv()

    def slot(way, s):
        if s == 0:
            return 0
        if s == mid:
            return mid
        return s if way == 0 else mid + s

    started = []

    def ring_copy(way, s, j):
        return remote(
            buf.at[slot(way, s), j, k], buf.at[slot(way, s + 1), j, k],
            ring_send.at[way, s, j], ring_recv.at[way, s, j], right if way == 0 else left,
        )

    def core_copy(sl, j):
        return remote(buf.at[sl, j, k], buf.at[sl, j, k], core_send.at[sl, j], core_recv.at[sl, j], core_peer)

    def start(copy):
        copy.start()
        started.append(copy)

    def core_wait(sl):
        for j in range(2):
            remote(
                buf.at[sl, j, 1 - k], buf.at[sl, j, 1 - k], core_send.at[sl, j], core_recv.at[sl, j], core_peer
            ).wait_recv()

    for step in range(2):
        for way in range(2):
            j = step if way == 0 else 1 - step
            if mid > 1 or step == 0:
                start(ring_copy(way, 0, j))
    for j in range(2):
        start(core_copy(0, j))

    for j in range(2):
        gate = jnp.dot(feat, wmod[:, 2 * D + j * half:2 * D + (j + 1) * half], preferred_element_type=jnp.float32)
        negate[j] = -gap * gate
        drift[j] = -gap * latent_ref[0, :, j * half:(j + 1) * half]

    score_scale = HD ** (-0.5) * math.log2(math.e)
    tiles = half // (2 * HD)
    n_rows = 2 * Rp

    def frames_of(sl):
        last = buf[sl, 0, 0, Rp - 16:Rp, :].astype(jnp.float32) + buf[sl, 0, 1, Rp - 16:Rp, :].astype(jnp.float32)
        place = R - (Rp - 16)
        return last[place:place + 1, :n_rows]

    def head_norm(rows):
        return (rows * lax.rsqrt(jnp.mean(rows * rows, axis=-1, keepdims=True) + norm_eps)).astype(jnp.bfloat16)

    def project(sl, i, j):
        cols = pl.ds(pl.multiple_of(j * 2 * HD, 2 * HD), 2 * HD)
        one = jnp.dot(
            buf[sl, 0].reshape(n_rows, half), wqkv[i, 0:half, cols], preferred_element_type=jnp.float32
        )
        return one + jnp.dot(
            buf[sl, 1].reshape(n_rows, half), wqkv[i, half:D, cols], preferred_element_type=jnp.float32
        )

    def attend(sl, query_frame):
        key_frame = frames_of(sl)
        ones = jnp.ones((n_rows, HD), jnp.bfloat16)

        def tile(j, carry):
            if sl == 0:
                qq = project(sl, 0, j)
                for g in range(2):
                    qbuf[j, g] = head_norm(qq[:, g * HD:(g + 1) * HD])
            kk = project(sl, 1, j)
            vv = project(sl, 2, j)
            allowed = key_frame <= query_frame
            for g in range(2):
                key = head_norm(kk[:, g * HD:(g + 1) * HD])
                value = jnp.concatenate([vv[:, g * HD:(g + 1) * HD].astype(jnp.bfloat16), ones], axis=1)
                scores = lax.dot_general(
                    qbuf[j, g], key, (((1,), (1,)), ((), ())), preferred_element_type=jnp.float32
                )
                weights = jnp.where(allowed, jnp.exp2(scores * score_scale), 0.0).astype(jnp.bfloat16)
                part = jnp.dot(weights, value, preferred_element_type=jnp.float32)
                if sl == 0:
                    acc[j, g] = part
                else:
                    acc[j, g] += part
            return carry

        lax.fori_loop(0, tiles, tile, 0)

    core_wait(0)
    own_frame = frames_of(0)
    diagonal = lax.broadcasted_iota(jnp.int32, (n_rows, n_rows), 0) == lax.broadcasted_iota(
        jnp.int32, (n_rows, n_rows), 1
    )
    query_frame = jnp.sum(jnp.where(diagonal, own_frame, 0.0), axis=1, keepdims=True)
    for i in range(3):
        loads[1 + i].wait()
    attend(0, query_frame)

    for s in range(1, mid + 1):
        for step in range(2):
            for way in range(2):
                j = step if way == 0 else 1 - step
                if s == mid and step == 1:
                    continue
                ring_copy(way, s - 1, j).wait_recv()
                if s < mid - 1 or (s == mid - 1 and step == 0):
                    start(ring_copy(way, s, j))
                start(core_copy(slot(way, s), j))
        if s < mid:
            for way in range(2):
                core_wait(slot(way, s))
                attend(slot(way, s), query_frame)
        else:
            core_wait(mid)
            attend(mid, query_frame)

    def att_copy(b):
        return remote(
            atts.at[b], attr.at[k], att_send.at[b], att_recv.at[k], {"tm": 2 * a + h, "ctx": b * ring + r}
        )

    for b in range(2):
        for j in range(tiles):
            for g in range(2):
                top = acc[j, g, b * Rp:(b + 1) * Rp, 0:HD]
                bottom = acc[j, g, b * Rp:(b + 1) * Rp, HD:2 * HD]
                first = (2 * j + g) * HD
                atts[b, :, first:first + HD] = (top / bottom).astype(jnp.bfloat16)
        mine = jnp.logical_and(k == h, k == b)

        @pl.when(mine)
        def _():
            attr[k] = atts[b]

        @pl.when(jnp.logical_not(mine))
        def _():
            att_copy(b).start()

    for i in range(2):
        @pl.when(jnp.logical_not(jnp.logical_and(k == h, k == i)))
        def _():
            remote(
                atts.at[i], attr.at[i], att_send.at[i], att_recv.at[i], {"tm": 2 * a + i, "ctx": k * ring + r}
            ).wait_recv()

    loads[4].wait()
    for j in range(2):
        branch = jnp.zeros((Rp, half), jnp.float32)
        for i in range(2):
            branch += jnp.dot(
                attr[i], wo[i * half:(i + 1) * half, j * half:(j + 1) * half], preferred_element_type=jnp.float32
            )
        drift[j] += negate[j] * branch[:R]
        start(remote(drift.at[j], pdrift.at[j], d_send.at[j], d_recv.at[j], core_peer))
    for j in range(2):
        remote(drift.at[j], pdrift.at[j], d_send.at[j], d_recv.at[j], core_peer).wait_recv()

    def x_copy(d):
        return remote(xsend, xrecv.at[d - 1], x_send.at[d - 1], x_recv.at[d - 1], {"tm": 2 * ((a + d) % pairs) + k})

    xsend[...] = drift[k] + pdrift[k]
    for d in range(1, pairs):
        @pl.when(a + d < pairs)
        def _():
            x_copy(d).start()

    e_copy = remote(etot.at[k], etot.at[k], e_send, e_recv, core_peer)
    e_landed = remote(etot.at[1 - k], etot.at[1 - k], e_send, e_recv, core_peer)
    for j in range(2):
        js = slice(j * half, (j + 1) * half)
        here = anchor_ref[:, js] + drift[j]
        out_ref[0, :, js] = jnp.where(k == 1, here + pdrift[j], here)

    @pl.when(a > 0)
    def _():
        etot[k] = jnp.zeros((R, half), jnp.float32)

    for d in range(1, pairs):
        @pl.when(a >= d)
        def _():
            x_copy(d).wait_recv()
            etot[k] += xrecv[d - 1]

    @pl.when(a > 0)
    def _():
        e_copy.start()
        e_landed.wait_recv()
        for j in range(2):
            js = slice(j * half, (j + 1) * half)
            out_ref[0, :, js] += etot[j]
        e_copy.wait_send()

    for copy in started:
        copy.wait_send()

    @pl.when(k != h)
    def _():
        for j in range(2):
            swap_copy(j).wait_send()

    for b in range(2):
        @pl.when(jnp.logical_not(jnp.logical_and(k == h, k == b)))
        def _():
            att_copy(b).wait_send()

    for d in range(1, pairs):
        @pl.when(a + d < pairs)
        def _():
            x_copy(d).wait_send()


def per_device(tm_size, ctx_size, iterate, anchor, frame_index, noise_steps, qkv_weight, out_weight, mod_weight):
    R, D = anchor.shape
    half = D // 2
    ring = ctx_size // 2
    pairs = tm_size // 2
    mid = ring // 2
    Rp = (R + 1 + 15) // 16 * 16
    features, gap = token_terms(noise_steps[0], frame_index, mod_weight.shape[0])
    never = float(4 * noise_steps.shape[1])
    frames = jnp.concatenate([frame_index.astype(jnp.float32), jnp.full((Rp - R,), never, jnp.float32)])
    zero = jnp.zeros_like(frames)
    high = lax.axis_index("ctx") // ring
    pair_row = jnp.concatenate([jnp.where(high == 0, frames, zero), jnp.where(high == 1, frames, zero)])
    frame_rows = jnp.pad(pair_row[None, :], ((0, Rp - R - 1), (0, half - 2 * Rp)))
    vmem = pl.BlockSpec(memory_space=pltpu.VMEM)
    hbm = pl.BlockSpec(memory_space=pl.ANY)
    dma = pltpu.SemaphoreType.DMA
    return pl.pallas_call(
        functools.partial(kernel, tm_size, ctx_size),
        out_shape=jax.ShapeDtypeStruct((1, R, D), jnp.float32),
        in_specs=[vmem] * 5 + [hbm] * 3,
        out_specs=vmem,
        scratch_shapes=[
            pltpu.VMEM((3, D, half), jnp.bfloat16),
            pltpu.VMEM((D, D), jnp.bfloat16),
            pltpu.VMEM(mod_weight.shape, jnp.bfloat16),
            pltpu.VMEM((2, Rp, half), jnp.bfloat16),
            pltpu.VMEM((ring, 2, 2, Rp, half), jnp.bfloat16),
            pltpu.VMEM((half // (2 * HD), 2, 2 * Rp, HD), jnp.bfloat16),
            pltpu.VMEM((half // (2 * HD), 2, 2 * Rp, 2 * HD), jnp.float32),
            pltpu.VMEM((2, Rp, half), jnp.bfloat16),
            pltpu.VMEM((2, Rp, half), jnp.bfloat16),
            pltpu.VMEM((2, R, half), jnp.float32),
            pltpu.VMEM((2, R, half), jnp.float32),
            pltpu.VMEM((2, R, half), jnp.float32),
            pltpu.VMEM((R, half), jnp.float32),
            pltpu.VMEM((max(pairs - 1, 1), R, half), jnp.float32),
            pltpu.VMEM((2, R, half), jnp.float32),
            dma((5,)),
            dma((2,)), dma((2,)),
            dma((2, mid, 2)), dma((2, mid, 2)),
            dma((ring, 2)), dma((ring, 2)),
            dma((2,)), dma((2,)),
            dma((2,)), dma((2,)),
            dma((max(pairs - 1, 1),)), dma((max(pairs - 1, 1),)),
            dma, dma,
        ],
        compiler_params=pltpu.CompilerParams(
            collective_id=0, has_side_effects=True, vmem_limit_bytes=56 * 1024 * 1024
        ),
    )(iterate, anchor, features, gap, frame_rows, qkv_weight, out_weight, mod_weight)


def solution(mesh):
    placed = (P("tm", "ctx", None), P("ctx", None), P("ctx"), P("tm", None), P(), P(), P())
    return jax.shard_map(
        functools.partial(per_device, mesh.shape["tm"], mesh.shape["ctx"]),
        mesh=mesh, in_specs=placed, out_specs=P("tm", "ctx", None), check_vma=False,
    )
```

time: 236 us -> 78.6 us (0.33)
  waiting for transfers between devices: 86.1 us -> 0 us
  Pallas kernels: 0 us -> 72.1 us
  matrix products: 46.7 us -> 0 us
  local copies, waits for them, and re-layouts: 45.5 us -> 3.63 us
  other arithmetic: 30.7 us -> 2.6 us
  between operations: 14.3 us -> 0.02 us
  blocking collectives: 11 us -> 0 us
    all_gather x2 -> x0, waiting for transfers between devices: 86.1 us -> none  [the longest x1 53.1 us: velocity_drift(): lax.all_gather(normed, 'ctx', axis=0, tiled=True)]
    pallas_call x0 -> x1, Pallas kernels: none -> 72.1 us  [per_device(): pl.pallas_call(functools.partial(kernel, tm_size, ctx_size), out_shape=ja...]
    dot_general x8 -> x0, matrix products: 46.7 us -> none  [the longest x1 17.1 us: velocity_drift(): jnp.dot(lax.all_gather(normed, 'ctx', axis=0, tiled=True), kv_weight, pre...]
    mul x5 -> x0, local copies, waits for them, and re-layouts: 23.6 us -> none  [the longest x3 13.2 us: head_norm(): split * lax.rsqrt(jnp.mean(split * split, axis=-1, keepdims=True) + norm_...]
    unnamed x1 -> x0, blocking collectives: 11 us -> none
    convert_element_type x2 -> x1, other arithmetic: 10.1 us -> 0.68 us  [per_device(): frame_index.astype(jnp.float32)]
    slice x2 -> x0, local copies, waits for them, and re-layouts: 9.05 us -> none  [velocity_drift(): values = kv_rows[:, model_width:].astype(jnp.bfloat16)]
    reduce_sum x4 -> x1, other arithmetic: 7.45 us -> 0.78 us  [token_terms(): jnp.sum(jnp.where(hit, steps_row[None, :], 0), axis=1).astype(jnp.float32)]
  transfers between devices with their start and end apart: 2 -> 0, of which waited for: 2 -> 0; matrix products, arithmetic and copies ran while one was open for 3% -> 0% of each run, Pallas kernels for 0% -> 0%
where the time goes in v1:
time: 78.6 us; the launch traced here: 78.3 us
  Pallas kernels  72.1 us (92%)
  local copies, waits for them, and re-layouts  3.63 us (5%)
  other arithmetic  2.6 us (3%)
    pallas_call x1, Pallas kernels, per_device(): pl.pallas_call(functools.partial(kernel, tm_size, ctx_size), out_shape=ja...  72.1 us
    unnamed x1, local copies, waits for them, and re-layouts  2.25 us

profile of v1, /device:TPU:3, one launch (start us, length us, event | category | flops | bytes accessed | tf_op | source)
XLA Modules:
  0.0 78.3 jit_solution(9799657117360007180)
XLA Ops:
  0.0 0.8 select_reduce_fusion
  0.8 0.7 convert_element_type.21
  1.5 0.1 pad_maximum_fusion.1
  1.6 0.6 pad.5.frow_ref
  2.2 0.4 fusion
  2.6 0.6 pad_maximum_fusion.feat_ref
  3.2 0.8 copy.9.gap_ref
  4.0 72.1 %shard_map.73 = f32[1,168,1536]{2,1,0:T(8,128)} custom-call(f32[1,168,1536]{2,1,0:T(8,128)} %latent_ref.1, f32[168,1536]{1,0:T(8,128)} %anchor_ref.1, bf16[168,256]{1,0:T(8,128)(2,1)} %pad_maximum_fusion.feat_ref, f32[168,1]{1,0:T(8,128)} %copy.9.gap_ref, f32[8,768]{1,0:T(8,128)} %pad.5.frow_ref, bf16[1536,4608]{1,0:T(8,128)(2,1)} %qkv_ref.1, ...), custom_call_target="tpu_custom_call" | custom-call | tf_op jit(solution)/shard_map/pallas_call | solution.py:360
  76.1 2.2 %copy.11 = f32[1,168,1536]{2,1,0:T(8,128)} copy(f32[1,168,1536]{2,1,0:T(8,128)} %shard_map.73) | data formatting | bytes 2064384
  (5 shorter events, 0.0 us)

commit v2 on v1

v2 whole, which is shorter than its diff:
```python
import functools
import math

import jax
import jax.numpy as jnp
from jax import lax
from jax.experimental import pallas as pl
from jax.experimental.pallas import tpu as pltpu
from jax.sharding import PartitionSpec as P

HD = 128
NSCHED = 12
MESH = pl.DeviceIdType.MESH

shift_factor = 5.0
norm_eps = 1e-06


def noise_level(level_index):
    fraction = level_index / NSCHED
    return shift_factor * fraction / (1.0 + (shift_factor - 1.0) * fraction)


def token_terms(steps_row, frame_index, freq):
    frame_count = steps_row.shape[0]
    hit = frame_index[:, None] == jnp.arange(frame_count, dtype=jnp.int32)[None, :]
    level_index = jnp.sum(jnp.where(hit, steps_row[None, :], 0), axis=1).astype(jnp.float32)
    upper = noise_level(level_index + 1.0)
    lower = noise_level(level_index)
    half_freq = freq // 2
    rates = jnp.exp(-math.log(10000.0) * jnp.arange(half_freq, dtype=jnp.float32) / half_freq)
    angles = (1000.0 * upper)[:, None] * rates[None, :]
    features = jnp.concatenate([jnp.cos(angles), jnp.sin(angles)], axis=1).astype(jnp.bfloat16)
    return features, (upper - lower)[:, None]


CHUNKS = 3


def kernel(
    tm_size, ctx_size,
    latent_ref, feat_ref, gap_ref, frow_ref, qkv_ref, wo_ref, mod_ref,
    out_ref,
    wqkv, wo, wmod, own, buf, qbuf, qframe, acc, kbuf, vbuf, atts, attr, negate, local, plocal, base, drift,
    db, pdb, xa, xar, yar, xs, xr, yr,
    w_sem, swap_send, swap_recv, ring_send, ring_recv, opp_send, opp_recv, core_send, core_recv,
    att_send, att_recv, n_send, n_recv, d_send, d_recv, xa_send, xa_recv, ya_send, ya_recv,
    x_send, x_recv, y_send, y_recv,
):
    R, D = latent_ref.shape[1], latent_ref.shape[2]
    half = D // 2
    wide = D // CHUNKS
    Rp = own.shape[1]
    ring = ctx_size // 2
    pairs = tm_size // 2
    mid = ring // 2
    t = lax.axis_index("tm")
    c = lax.axis_index("ctx")
    a, k = t // 2, t % 2
    h, r = c // ring, c % ring
    u = r // 2
    p = 2 * u + (r % 2 + u) % 2

    def at_ring(q):
        v = q // 2
        return h * ring + 2 * v + (q % 2 + v) % 2

    core_peer = {"tm": 2 * a + 1 - k}
    swap_peer = {"tm": 2 * a + h, "ctx": k * ring + r}
    right = {"ctx": at_ring((p + 1) % ring)}
    left = {"ctx": at_ring((p + ring - 1) % ring)}
    pair_peer = {"ctx": at_ring(p + 1 - 2 * (p % 2))}

    loads = [pltpu.make_async_copy(mod_ref, wmod, w_sem.at[0])]
    for i in range(3):
        col = pl.multiple_of(i * D + k * half, 128)
        loads.append(pltpu.make_async_copy(qkv_ref.at[:, pl.ds(col, half)], wqkv.at[i], w_sem.at[1 + i]))
    loads.append(pltpu.make_async_copy(wo_ref, wo, w_sem.at[4]))
    for load in loads:
        load.start()

    barrier = pltpu.get_barrier_semaphore()
    greeted = [
        core_peer,
        {"tm": 2 * a + k, "ctx": (1 - h) * ring + r},
        {"tm": 2 * a + 1 - k, "ctx": (1 - h) * ring + r},
        left,
        right,
    ]
    for d in range(1, pairs):
        greeted.append({"tm": 2 * ((a + d) % pairs) + k})
    for peer in greeted:
        pl.semaphore_signal(barrier, inc=1, device_id=peer, device_id_type=MESH)

    def remote(src, dst, s_sem, r_sem, peer):
        return pltpu.make_async_remote_copy(
            src_ref=src, dst_ref=dst, send_sem=s_sem, recv_sem=r_sem, device_id=peer, device_id_type=MESH
        )

    started = []

    def start(copy):
        copy.start()
        started.append(copy)

    def swap_copy(j):
        return remote(own.at[j], buf.at[0, j, h], swap_send.at[j], swap_recv.at[j], swap_peer)

    def swap_landed(j):
        return remote(own.at[j], buf.at[0, j, k], swap_send.at[j], swap_recv.at[j], swap_peer)

    x = latent_ref[0]
    center = x - jnp.mean(x, axis=-1, keepdims=True)
    spread = jnp.mean(center * center, axis=-1, keepdims=True)
    unit = center * lax.rsqrt(spread + norm_eps)
    loads[0].wait()
    feat = feat_ref[...]
    gap = gap_ref[...]
    for j in range(CHUNKS):
        lo, hi = j * wide, (j + 1) * wide
        shift = jnp.dot(feat, wmod[:, lo:hi], preferred_element_type=jnp.float32)
        scale = jnp.dot(feat, wmod[:, D + lo:D + hi], preferred_element_type=jnp.float32)
        rows = unit[:, lo:hi] * (1.0 + scale[:R]) + shift[:R]
        tail = frow_ref[...] if j == 0 else jnp.zeros((Rp - R, wide), jnp.float32)
        own[j] = jnp.concatenate([rows, tail], axis=0).astype(jnp.bfloat16)
        if j == 0:
            pl.semaphore_wait(barrier, len(greeted))

        @pl.when(k != h)
        def _():
            swap_copy(j).start()

        @pl.when(k == h)
        def _():
            buf[0, j, k] = own[j]

    def slot(way, s):
        if s == 0:
            return 0
        if s == mid:
            return mid
        return s if way == 0 else mid + s

    def ring_copy(way, s, j):
        return remote(
            buf.at[slot(way, s), j, k], buf.at[slot(way, s + 1), j, k],
            ring_send.at[way, s, j], ring_recv.at[way, s, j], right if way == 0 else left,
        )

    def opposite_copy():
        source = jnp.where(p % 2 == 0, slot(0, mid - 1), slot(1, mid - 1))
        return remote(buf.at[source, 1, k], buf.at[mid, 1, k], opp_send, opp_recv, pair_peer)

    def core_copy(sl, j):
        return remote(buf.at[sl, j, k], buf.at[sl, j, k], core_send.at[sl, j], core_recv.at[sl, j], core_peer)

    def core_wait(sl):
        for j in range(CHUNKS):
            remote(
                buf.at[sl, j, 1 - k], buf.at[sl, j, 1 - k], core_send.at[sl, j], core_recv.at[sl, j], core_peer
            ).wait_recv()

    for j in range(2):
        local[j] = -gap[:R] * latent_ref[0, :, j * half:(j + 1) * half]
        start(remote(local.at[j], plocal.at[j], n_send.at[j], n_recv.at[j], core_peer))

    for j in range(CHUNKS):
        @pl.when(k != h)
        def _():
            swap_landed(j).wait_recv()

        for way in range(2):
            start(ring_copy(way, 0, j))
        start(core_copy(0, j))

    for j in range(2):
        gate = jnp.dot(feat, wmod[:, 2 * D + j * half:2 * D + (j + 1) * half], preferred_element_type=jnp.float32)
        negate[j] = -gap * gate

    score_scale = HD ** (-0.5) * math.log2(math.e)
    tiles = half // (2 * HD)
    n_rows = 2 * Rp

    def frames_of(sl):
        last = buf[sl, 0, 0, Rp - 16:Rp, :].astype(jnp.float32) + buf[sl, 0, 1, Rp - 16:Rp, :].astype(jnp.float32)
        place = R - (Rp - 16)
        return last[place:place + 1, :n_rows]

    def head_norm(rows):
        return (rows * lax.rsqrt(jnp.mean(rows * rows, axis=-1, keepdims=True) + norm_eps)).astype(jnp.bfloat16)

    def project(sl, i, j):
        cols = pl.ds(pl.multiple_of(j * 2 * HD, 2 * HD), 2 * HD)
        total = None
        for m in range(CHUNKS):
            one = jnp.dot(
                buf[sl, m].reshape(n_rows, wide), wqkv[i, m * wide:(m + 1) * wide, cols],
                preferred_element_type=jnp.float32,
            )
            total = one if total is None else total + one
        return total

    def keys_values(sl, j):
        kk = project(sl, 1, j)
        vv = project(sl, 2, j)
        ones = jnp.ones((n_rows, HD), jnp.bfloat16)
        keys = [head_norm(kk[:, g * HD:(g + 1) * HD]) for g in range(2)]
        values = [
            jnp.concatenate([vv[:, g * HD:(g + 1) * HD].astype(jnp.bfloat16), ones], axis=1) for g in range(2)
        ]
        return keys, values

    def partial_sums(query, key, value, allowed):
        scores = lax.dot_general(query, key, (((1,), (1,)), ((), ())), preferred_element_type=jnp.float32)
        weights = jnp.where(allowed, jnp.exp2(scores * score_scale), 0.0).astype(jnp.bfloat16)
        return jnp.dot(weights, value, preferred_element_type=jnp.float32)

    def attend(sl):
        key_frame = frames_of(sl)

        def tile(j, carry):
            if sl == 0:
                qq = project(sl, 0, j)
                for g in range(2):
                    qbuf[j, g] = head_norm(qq[:, g * HD:(g + 1) * HD]).reshape(2, Rp, HD)
            keys, values = keys_values(sl, j)
            allowed = key_frame <= qframe[...].reshape(n_rows, 1)
            for g in range(2):
                part = partial_sums(qbuf[j, g].reshape(n_rows, HD), keys[g], values[g], allowed)
                part = part.reshape(2, Rp, 2 * HD)
                if sl == 0:
                    acc[j, g] = part
                else:
                    acc[j, g] += part
            return carry

        lax.fori_loop(0, tiles, tile, 0)

    core_wait(0)
    diagonal = lax.broadcasted_iota(jnp.int32, (n_rows, n_rows), 0) == lax.broadcasted_iota(
        jnp.int32, (n_rows, n_rows), 1
    )
    qframe[...] = jnp.sum(jnp.where(diagonal, frames_of(0), 0.0), axis=1, keepdims=True).reshape(2, Rp, 1)
    for i in range(3):
        loads[1 + i].wait()
    attend(0)

    def later(d):
        return {"tm": 2 * ((a + d) % pairs) + k}

    def xa_copy(d):
        return remote(xa, xar.at[d - 1], xa_send.at[d - 1], xa_recv.at[d - 1], later(d))

    def ya_copy(d):
        return remote(xar.at[d - 1], yar.at[d - 1], ya_send.at[d - 1], ya_recv.at[d - 1], core_peer)

    def x_copy(d):
        return remote(xs, xr.at[d - 1], x_send.at[d - 1], x_recv.at[d - 1], later(d))

    def y_copy(d):
        return remote(xr.at[d - 1], yr.at[d - 1], y_send.at[d - 1], y_recv.at[d - 1], core_peer)

    for j in range(2):
        remote(local.at[j], plocal.at[j], n_send.at[j], n_recv.at[j], core_peer).wait_recv()
    xa[...] = local[k] + plocal[k]
    for d in range(1, pairs):
        @pl.when(a + d < pairs)
        def _():
            xa_copy(d).start()

    for j in range(2):
        base[j] = jnp.where(k == 1, local[j] + plocal[j], local[j])

    for s in range(1, mid):
        for j in range(CHUNKS):
            for way in range(2):
                ring_copy(way, s - 1, j).wait_recv()
                if s < mid - 1 or (way == 0 and j == 0) or (way == 1 and j == CHUNKS - 1):
                    start(ring_copy(way, s, j))
                start(core_copy(slot(way, s), j))
            if s == mid - 1 and j == 1:
                start(opposite_copy())
        for way in range(2):
            core_wait(slot(way, s))
            attend(slot(way, s))

    for d in range(1, pairs):
        @pl.when(a >= d)
        def _():
            xa_copy(d).wait_recv()
            ya_copy(d).start()

    ring_copy(0, mid - 1, 0).wait_recv()
    start(core_copy(mid, 0))
    opposite_copy().wait_recv()
    start(core_copy(mid, 1))
    ring_copy(1, mid - 1, CHUNKS - 1).wait_recv()
    start(core_copy(mid, CHUNKS - 1))
    core_wait(mid)

    def last_tile(j, carry):
        keys, values = keys_values(mid, j)
        for g in range(2):
            kbuf[j, g] = keys[g]
            vbuf[j, g] = values[g]
        return carry

    lax.fori_loop(0, tiles, last_tile, 0)
    last_frame = frames_of(mid)

    def finish(b, m):
        allowed = last_frame <= qframe[b]
        for j in range(tiles):
            for g in range(2):
                full = acc[j, g, b] + partial_sums(qbuf[j, g, b], kbuf[j, g], vbuf[j, g], allowed)
                first = (2 * j + g) * HD
                atts[m, :, first:first + HD] = (full[:, :HD] / full[:, HD:]).astype(jnp.bfloat16)

    away = remote(
        atts.at[0], attr.at[k], att_send.at[0], att_recv.at[k], {"tm": 2 * a + h, "ctx": (1 - h) * ring + r}
    )
    across = remote(atts.at[1], attr.at[k], att_send.at[1], att_recv.at[k], core_peer)
    finish(1 - h, 0)
    start(away)
    finish(h, 1)

    @pl.when(k == h)
    def _():
        attr[k] = atts[1]

    @pl.when(k != h)
    def _():
        across.start()

    for d in range(1, pairs):
        @pl.when(a >= d)
        def _():
            ya_copy(d).wait_recv()
            base[k] += xar[d - 1]
            base[1 - k] += yar[d - 1]

    for i in range(2):
        @pl.when(jnp.logical_not(jnp.logical_and(k == h, k == i)))
        def _():
            remote(
                atts.at[i], attr.at[i], att_send.at[i], att_recv.at[i], {"tm": 2 * a + i, "ctx": k * ring + r}
            ).wait_recv()

    loads[4].wait()
    for j in range(2):
        branch = jnp.zeros((Rp, half), jnp.float32)
        for i in range(2):
            branch += jnp.dot(
                attr[i], wo[i * half:(i + 1) * half, j * half:(j + 1) * half], preferred_element_type=jnp.float32
            )
        drift[j] = negate[j] * branch
        db[j] = drift[j].astype(jnp.bfloat16)
        start(remote(db.at[j], pdb.at[j], d_send.at[j], d_recv.at[j], core_peer))
    for j in range(2):
        remote(db.at[j], pdb.at[j], d_send.at[j], d_recv.at[j], core_peer).wait_recv()

    xs[...] = (drift[k] + pdb[k].astype(jnp.float32)).astype(jnp.bfloat16)
    for d in range(1, pairs):
        @pl.when(a + d < pairs)
        def _():
            x_copy(d).start()

    for j in range(2):
        here = base[j] + drift[j, :R]
        base[j] = jnp.where(k == 1, here + pdb[j].astype(jnp.float32)[:R], here)

    for d in range(1, pairs):
        @pl.when(a >= d)
        def _():
            x_copy(d).wait_recv()
            y_copy(d).start()
            base[k] += xr[d - 1].astype(jnp.float32)[:R]
            y_copy(d).wait_recv()
            base[1 - k] += yr[d - 1].astype(jnp.float32)[:R]

    for j in range(2):
        out_ref[0, :, j * half:(j + 1) * half] = base[j]

    for copy in started:
        copy.wait_send()

    @pl.when(k != h)
    def _():
        for j in range(CHUNKS):
            swap_copy(j).wait_send()
        across.wait_send()

    for d in range(1, pairs):
        @pl.when(a + d < pairs)
        def _():
            xa_copy(d).wait_send()
            x_copy(d).wait_send()

        @pl.when(a >= d)
        def _():
            ya_copy(d).wait_send()
            y_copy(d).wait_send()


def per_device(tm_size, ctx_size, iterate, anchor, frame_index, noise_steps, qkv_weight, out_weight, mod_weight):
    R, D = anchor.shape
    half = D // 2
    wide = D // CHUNKS
    ring = ctx_size // 2
    pairs = tm_size // 2
    far = max(pairs - 1, 1)
    mid = ring // 2
    Rp = (R + 1 + 15) // 16 * 16
    tiles = half // (2 * HD)
    features, gap = token_terms(noise_steps[0], frame_index, mod_weight.shape[0])
    features = jnp.pad(features, ((0, Rp - R), (0, 0)))
    gap = jnp.pad(gap, ((0, Rp - R), (0, 0)))
    never = float(4 * noise_steps.shape[1])
    frames = jnp.concatenate([frame_index.astype(jnp.float32), jnp.full((Rp - R,), never, jnp.float32)])
    zero = jnp.zeros_like(frames)
    high = lax.axis_index("ctx") // ring
    pair_row = jnp.concatenate([jnp.where(high == 0, frames, zero), jnp.where(high == 1, frames, zero)])
    frame_rows = jnp.pad(pair_row[None, :], ((0, Rp - R - 1), (0, wide - 2 * Rp)))
    vmem = pl.BlockSpec(memory_space=pltpu.VMEM)
    hbm = pl.BlockSpec(memory_space=pl.ANY)
    dma = pltpu.SemaphoreType.DMA
    f32, bf16 = jnp.float32, jnp.bfloat16
    total = pl.pallas_call(
        functools.partial(kernel, tm_size, ctx_size),
        out_shape=jax.ShapeDtypeStruct((1, R, D), f32),
        in_specs=[vmem] * 4 + [hbm] * 3,
        out_specs=vmem,
        scratch_shapes=[
            pltpu.VMEM((3, D, half), bf16),
            pltpu.VMEM((D, D), bf16),
            pltpu.VMEM(mod_weight.shape, bf16),
            pltpu.VMEM((CHUNKS, Rp, wide), bf16),
            pltpu.VMEM((ring, CHUNKS, 2, Rp, wide), bf16),
            pltpu.VMEM((tiles, 2, 2, Rp, HD), bf16),
            pltpu.VMEM((2, Rp, 1), f32),
            pltpu.VMEM((tiles, 2, 2, Rp, 2 * HD), f32),
            pltpu.VMEM((tiles, 2, 2 * Rp, HD), bf16),
            pltpu.VMEM((tiles, 2, 2 * Rp, 2 * HD), bf16),
            pltpu.VMEM((2, Rp, half), bf16),
            pltpu.VMEM((2, Rp, half), bf16),
            pltpu.VMEM((2, Rp, half), f32),
            pltpu.VMEM((2, R, half), f32),
            pltpu.VMEM((2, R, half), f32),
            pltpu.VMEM((2, R, half), f32),
            pltpu.VMEM((2, Rp, half), f32),
            pltpu.VMEM((2, Rp, half), bf16),
            pltpu.VMEM((2, Rp, half), bf16),
            pltpu.VMEM((R, half), f32),
            pltpu.VMEM((far, R, half), f32),
            pltpu.VMEM((far, R, half), f32),
            pltpu.VMEM((Rp, half), bf16),
            pltpu.VMEM((far, Rp, half), bf16),
            pltpu.VMEM((far, Rp, half), bf16),
            dma((5,)),
            dma((CHUNKS,)), dma((CHUNKS,)),
            dma((2, mid, CHUNKS)), dma((2, mid, CHUNKS)),
            dma, dma,
            dma((ring, CHUNKS)), dma((ring, CHUNKS)),
            dma((2,)), dma((2,)),
            dma((2,)), dma((2,)),
            dma((2,)), dma((2,)),
            dma((far,)), dma((far,)),
            dma((far,)), dma((far,)),
            dma((far,)), dma((far,)),
            dma((far,)), dma((far,)),
        ],
        compiler_params=pltpu.CompilerParams(
            collective_id=0, has_side_effects=True, vmem_limit_bytes=56 * 1024 * 1024
        ),
    )(iterate, features, gap, frame_rows, qkv_weight, out_weight, mod_weight)
    return anchor[None] + total


def solution(mesh):
    placed = (P("tm", "ctx", None), P("ctx", None), P("ctx"), P("tm", None), P(), P(), P())
    return jax.shard_map(
        functools.partial(per_device, mesh.shape["tm"], mesh.shape["ctx"]),
        mesh=mesh, in_specs=placed, out_specs=P("tm", "ctx", None), check_vma=False,
    )
```

time: 78.6 us -> 71.5 us (0.910)
  Pallas kernels: 72.1 us -> 65 us
  other arithmetic: 2.6 us -> 4.9 us
  local copies, waits for them, and re-layouts: 3.63 us -> 1.38 us
    pallas_call x1, Pallas kernels: 72.1 us -> 65 us  [per_device(): pl.pallas_call(functools.partial(kernel, tm_size, ctx_size), out_shape=ja...]
    add x0 -> x1, other arithmetic: none -> 2.29 us  [per_device(): return anchor[None] + total]
    unnamed x1 -> x2, local copies, waits for them, and re-layouts: 2.25 us -> 0.01 us
where the time goes in v2:
time: 71.5 us; the launch traced here: 71.3 us
  Pallas kernels  65 us (91%)
  other arithmetic  4.9 us (7%)
  local copies, waits for them, and re-layouts  1.38 us (2%)
    pallas_call x1, Pallas kernels, per_device(): pl.pallas_call(functools.partial(kernel, tm_size, ctx_size), out_shape=ja...  65 us
    add x1, other arithmetic, per_device(): return anchor[None] + total  2.29 us

profile of v2, /device:TPU:3, one launch (start us, length us, event | category | flops | bytes accessed | tf_op | source)
XLA Modules:
  0.0 71.3 jit_solution(10520125609383142461)
XLA Ops:
  0.0 0.8 %select_reduce_fusion = s32[168]{0:T(256)S(1)} fusion(s32[8]{0:T(128)} %bitcast.5, s32[168]{0:T(256)} %param.9), kind=kLoop, calls=%fused_computation.9 | loop fusion | flops 3864 | bytes 1376 | tf_op jit(solution)/shard_map/reduce_sum | solution.py:27
  0.8 0.7 convert_element_type.25
  1.5 0.1 pad_maximum_fusion
  1.6 0.6 pad.15.frow_ref
  2.2 0.4 fusion.3
  2.6 0.7 fusion.2.feat_ref
  3.2 0.1 copy.9
  3.3 0.7 pad.14.gap_ref
  4.0 0.0 copy-start
  4.0 65.0 %shard_map.73 = f32[1,168,1536]{2,1,0:T(8,128)} custom-call(f32[1,168,1536]{2,1,0:T(8,128)} %latent_ref.1, bf16[176,256]{1,0:T(8,128)(2,1)} %fusion.2.feat_ref, f32[176,1]{1,0:T(8,128)} %pad.14.gap_ref, f32[8,512]{1,0:T(8,128)} %pad.15.frow_ref, bf16[1536,4608]{1,0:T(8,128)(2,1)} %qkv_ref.1, bf16[1536,1536]{1,0:T(8,128)(2,1)} %wo_ref.1, ...), custom_call_target="tpu_custom_call" | custom-call | tf_op jit(solution)/shard_map/pallas_call | solution.py:428
  69.0 0.0 copy-done
  69.0 2.3 %bitcast_add_fusion = f32[1,168,1536]{2,1,0:T(8,128)} fusion(f32[1,168,1536]{2,1,0:T(8,128)} %shard_map.73, f32[168,1536]{1,0:T(8,128)S(1)} %copy-done), kind=kLoop, calls=%fused_computation | loop fusion | flops 258048 | bytes 3096576 | tf_op jit(solution)/shard_map/add | solution.py:476
  (5 shorter events, 0.0 us)
Async XLA Ops:
  4.0 65.0 %copy-start = (f32[168,1536]{1,0:T(8,128)S(1)}, f32[168,1536]{1,0:T(8,128)}, u32[]{:S(2)}) copy-start(f32[168,1536]{1,0:T(8,128)} %param.8) | copy-start | bytes 3096580

commit v3 on v2

--- a/solution.py
+++ b/solution.py
@@ -21,25 +21,12 @@
     return shift_factor * fraction / (1.0 + (shift_factor - 1.0) * fraction)
 
 
-def token_terms(steps_row, frame_index, freq):
-    frame_count = steps_row.shape[0]
-    hit = frame_index[:, None] == jnp.arange(frame_count, dtype=jnp.int32)[None, :]
-    level_index = jnp.sum(jnp.where(hit, steps_row[None, :], 0), axis=1).astype(jnp.float32)
-    upper = noise_level(level_index + 1.0)
-    lower = noise_level(level_index)
-    half_freq = freq // 2
-    rates = jnp.exp(-math.log(10000.0) * jnp.arange(half_freq, dtype=jnp.float32) / half_freq)
-    angles = (1000.0 * upper)[:, None] * rates[None, :]
-    features = jnp.concatenate([jnp.cos(angles), jnp.sin(angles)], axis=1).astype(jnp.bfloat16)
-    return features, (upper - lower)[:, None]
-
-
 CHUNKS = 3
 
 
 def kernel(
     tm_size, ctx_size,
-    latent_ref, feat_ref, gap_ref, frow_ref, qkv_ref, wo_ref, mod_ref,
+    latent_ref, frame_ref, steps_ref, qkv_ref, wo_ref, mod_ref,
     out_ref,
     wqkv, wo, wmod, own, buf, qbuf, qframe, acc, kbuf, vbuf, atts, attr, negate, local, plocal, base, drift,
     db, pdb, xa, xar, yar, xs, xr, yr,
@@ -76,8 +63,7 @@
         col = pl.multiple_of(i * D + k * half, 128)
         loads.append(pltpu.make_async_copy(qkv_ref.at[:, pl.ds(col, half)], wqkv.at[i], w_sem.at[1 + i]))
     loads.append(pltpu.make_async_copy(wo_ref, wo, w_sem.at[4]))
-    for load in loads:
-        load.start()
+    loads[0].start()
 
     barrier = pltpu.get_barrier_semaphore()
     greeted = [
@@ -113,15 +99,38 @@
     center = x - jnp.mean(x, axis=-1, keepdims=True)
     spread = jnp.mean(center * center, axis=-1, keepdims=True)
     unit = center * lax.rsqrt(spread + norm_eps)
+
+    row_place = lax.broadcasted_iota(jnp.int32, (Rp, R), 0)
+    lane_place = lax.broadcasted_iota(jnp.int32, (Rp, R), 1)
+    frame_row = frame_ref[...].astype(jnp.float32)
+    frame_col = jnp.sum(jnp.where(row_place == lane_place, frame_row, 0.0), axis=1, keepdims=True)
+    level_index = jnp.zeros((Rp, 1), jnp.float32)
+    for f in range(steps_ref.shape[1]):
+        level_index += jnp.where(frame_col == float(f), steps_ref[0, f].astype(jnp.float32), 0.0)
+    upper = noise_level(level_index + 1.0)
+    gap = upper - noise_level(level_index)
+    half_freq = mod_ref.shape[0] // 2
+    rate_place = lax.broadcasted_iota(jnp.int32, (1, half_freq), 1).astype(jnp.float32)
+    rates = jnp.exp(-math.log(10000.0) * rate_place / half_freq)
+    angles = (1000.0 * upper) * rates
+    feat = jnp.concatenate([jnp.cos(angles), jnp.sin(angles)], axis=1).astype(jnp.bfloat16)
+    here_row = lax.broadcasted_iota(jnp.int32, (Rp, wide), 0)
+    here_lane = lax.broadcasted_iota(jnp.int32, (Rp, wide), 1)
+    never = float(4 * steps_ref.shape[1])
+    told = jnp.where(here_row < R, frame_col, never)
+    frames_out = jnp.sum(jnp.where(here_lane == here_row + h * Rp, told, 0.0), axis=0, keepdims=True)
+    spare_row = lax.broadcasted_iota(jnp.int32, (Rp - R, wide), 0)
+    frames_tail = jnp.where(spare_row == 0, frames_out, 0.0)
+
     loads[0].wait()
-    feat = feat_ref[...]
-    gap = gap_ref[...]
+    for load in loads[1:]:
+        load.start()
     for j in range(CHUNKS):
         lo, hi = j * wide, (j + 1) * wide
         shift = jnp.dot(feat, wmod[:, lo:hi], preferred_element_type=jnp.float32)
         scale = jnp.dot(feat, wmod[:, D + lo:D + hi], preferred_element_type=jnp.float32)
         rows = unit[:, lo:hi] * (1.0 + scale[:R]) + shift[:R]
-        tail = frow_ref[...] if j == 0 else jnp.zeros((Rp - R, wide), jnp.float32)
+        tail = frames_tail if j == 0 else jnp.zeros((Rp - R, wide), jnp.float32)
         own[j] = jnp.concatenate([rows, tail], axis=0).astype(jnp.bfloat16)
         if j == 0:
             pl.semaphore_wait(barrier, len(greeted))
@@ -254,11 +263,21 @@
     def ya_copy(d):
         return remote(xar.at[d - 1], yar.at[d - 1], ya_send.at[d - 1], ya_recv.at[d - 1], core_peer)
 
-    def x_copy(d):
-        return remote(xs, xr.at[d - 1], x_send.at[d - 1], x_recv.at[d - 1], later(d))
-
-    def y_copy(d):
-        return remote(xr.at[d - 1], yr.at[d - 1], y_send.at[d - 1], y_recv.at[d - 1], core_peer)
+    first_rows = (Rp // 2 + 15) // 16 * 16
+    bands = [(0, first_rows), (first_rows, Rp)]
+
+    def band(ref, i):
+        return ref.at[bands[i][0]:bands[i][1]]
+
+    def x_copy(d, i):
+        return remote(
+            band(xs, i), band(xr.at[d - 1], i), x_send.at[d - 1, i], x_recv.at[d - 1, i], later(d)
+        )
+
+    def y_copy(d, i):
+        return remote(
+            band(xr.at[d - 1], i), band(yr.at[d - 1], i), y_send.at[d - 1, i], y_recv.at[d - 1, i], core_peer
+        )
 
     for j in range(2):
         remote(local.at[j], plocal.at[j], n_send.at[j], n_recv.at[j], core_peer).wait_recv()
@@ -308,30 +327,41 @@
     lax.fori_loop(0, tiles, last_tile, 0)
     last_frame = frames_of(mid)
 
-    def finish(b, m):
-        allowed = last_frame <= qframe[b]
+    def finish(b, m, i):
+        lo, hi = bands[i]
+        allowed = last_frame <= qframe[b, lo:hi]
         for j in range(tiles):
             for g in range(2):
-                full = acc[j, g, b] + partial_sums(qbuf[j, g, b], kbuf[j, g], vbuf[j, g], allowed)
+                part = partial_sums(qbuf[j, g, b, lo:hi], kbuf[j, g], vbuf[j, g], allowed)
+                full = acc[j, g, b, lo:hi] + part
                 first = (2 * j + g) * HD
-                atts[m, :, first:first + HD] = (full[:, :HD] / full[:, HD:]).astype(jnp.bfloat16)
-
-    away = remote(
-        atts.at[0], attr.at[k], att_send.at[0], att_recv.at[k], {"tm": 2 * a + h, "ctx": (1 - h) * ring + r}
-    )
-    across = remote(atts.at[1], attr.at[k], att_send.at[1], att_recv.at[k], core_peer)
-    finish(1 - h, 0)
-    start(away)
-    finish(h, 1)
+                atts[m, lo:hi, first:first + HD] = (full[:, :HD] / full[:, HD:]).astype(jnp.bfloat16)
+
+    def away(i):
+        return remote(
+            band(atts.at[0], i), band(attr.at[k], i), att_send.at[0, i], att_recv.at[k, i],
+            {"tm": 2 * a + h, "ctx": (1 - h) * ring + r},
+        )
+
+    def across(i):
+        return remote(
+            band(atts.at[1], i), band(attr.at[k], i), att_send.at[1, i], att_recv.at[k, i], core_peer
+        )
+
+    for i in range(2):
+        finish(1 - h, 0, i)
+        start(away(i))
+    for i in range(2):
+        finish(h, 1, i)
+
+        @pl.when(k != h)
+        def _():
+            across(i).start()
 
     @pl.when(k == h)
     def _():
         attr[k] = atts[1]
 
-    @pl.when(k != h)
-    def _():
-        across.start()
-
     for d in range(1, pairs):
         @pl.when(a >= d)
         def _():
@@ -339,31 +369,38 @@
             base[k] += xar[d - 1]
             base[1 - k] += yar[d - 1]
 
+    loads[4].wait()
+
+    def d_copy(j, i):
+        return remote(band(db.at[j], i), band(pdb.at[j], i), d_send.at[j, i], d_recv.at[j, i], core_peer)
+
     for i in range(2):
-        @pl.when(jnp.logical_not(jnp.logical_and(k == h, k == i)))
-        def _():
-            remote(
-                atts.at[i], attr.at[i], att_send.at[i], att_recv.at[i], {"tm": 2 * a + i, "ctx": k * ring + r}
-            ).wait_recv()
-
-    loads[4].wait()
-    for j in range(2):
-        branch = jnp.zeros((Rp, half), jnp.float32)
-        for i in range(2):
-            branch += jnp.dot(
-                attr[i], wo[i * half:(i + 1) * half, j * half:(j + 1) * half], preferred_element_type=jnp.float32
-            )
-        drift[j] = negate[j] * branch
-        db[j] = drift[j].astype(jnp.bfloat16)
-        start(remote(db.at[j], pdb.at[j], d_send.at[j], d_recv.at[j], core_peer))
-    for j in range(2):
-        remote(db.at[j], pdb.at[j], d_send.at[j], d_recv.at[j], core_peer).wait_recv()
-
-    xs[...] = (drift[k] + pdb[k].astype(jnp.float32)).astype(jnp.bfloat16)
-    for d in range(1, pairs):
-        @pl.when(a + d < pairs)
-        def _():
-            x_copy(d).start()
+        lo, hi = bands[i]
+        for m in range(2):
+            @pl.when(jnp.logical_not(jnp.logical_and(k == h, k == m)))
+            def _():
+                remote(
+                    band(atts.at[m], i), band(attr.at[m], i), att_send.at[m, i], att_recv.at[m, i],
+                    {"tm": 2 * a + m, "ctx": k * ring + r},
+                ).wait_recv()
+
+        for j in range(2):
+            branch = jnp.zeros((hi - lo, half), jnp.float32)
+            for m in range(2):
+                branch += jnp.dot(
+                    attr[m, lo:hi], wo[m * half:(m + 1) * half, j * half:(j + 1) * half],
+                    preferred_element_type=jnp.float32,
+                )
+            drift[j, lo:hi] = negate[j, lo:hi] * branch
+            db[j, lo:hi] = drift[j, lo:hi].astype(jnp.bfloat16)
+            start(d_copy(j, i))
+        for j in range(2):
+            d_copy(j, i).wait_recv()
+        xs[lo:hi] = (drift[k, lo:hi] + pdb[k, lo:hi].astype(jnp.float32)).astype(jnp.bfloat16)
+        for d in range(1, pairs):
+            @pl.when(a + d < pairs)
+            def _():
+                x_copy(d, i).start()
 
     for j in range(2):
         here = base[j] + drift[j, :R]
@@ -372,10 +409,12 @@
     for d in range(1, pairs):
         @pl.when(a >= d)
         def _():
-            x_copy(d).wait_recv()
-            y_copy(d).start()
+            for i in range(2):
+                x_copy(d, i).wait_recv()
+                y_copy(d, i).start()
             base[k] += xr[d - 1].astype(jnp.float32)[:R]
-            y_copy(d).wait_recv()
+            for i in range(2):
+                y_copy(d, i).wait_recv()
             base[1 - k] += yr[d - 1].astype(jnp.float32)[:R]
 
     for j in range(2):
@@ -388,18 +427,21 @@
     def _():
         for j in range(CHUNKS):
             swap_copy(j).wait_send()
-        across.wait_send()
+        for i in range(2):
+            across(i).wait_send()
 
     for d in range(1, pairs):
         @pl.when(a + d < pairs)
         def _():
             xa_copy(d).wait_send()
-            x_copy(d).wait_send()
+            for i in range(2):
+                x_copy(d, i).wait_send()
 
         @pl.when(a >= d)
         def _():
             ya_copy(d).wait_send()
-            y_copy(d).wait_send()
+            for i in range(2):
+                y_copy(d, i).wait_send()
 
 
 def per_device(tm_size, ctx_size, iterate, anchor, frame_index, noise_steps, qkv_weight, out_weight, mod_weight):
@@ -412,15 +454,6 @@
     mid = ring // 2
     Rp = (R + 1 + 15) // 16 * 16
     tiles = half // (2 * HD)
-    features, gap = token_terms(noise_steps[0], frame_index, mod_weight.shape[0])
-    features = jnp.pad(features, ((0, Rp - R), (0, 0)))
-    gap = jnp.pad(gap, ((0, Rp - R), (0, 0)))
-    never = float(4 * noise_steps.shape[1])
-    frames = jnp.concatenate([frame_index.astype(jnp.float32), jnp.full((Rp - R,), never, jnp.float32)])
-    zero = jnp.zeros_like(frames)
-    high = lax.axis_index("ctx") // ring
-    pair_row = jnp.concatenate([jnp.where(high == 0, frames, zero), jnp.where(high == 1, frames, zero)])
-    frame_rows = jnp.pad(pair_row[None, :], ((0, Rp - R - 1), (0, wide - 2 * Rp)))
     vmem = pl.BlockSpec(memory_space=pltpu.VMEM)
     hbm = pl.BlockSpec(memory_space=pl.ANY)
     dma = pltpu.SemaphoreType.DMA
@@ -428,7 +461,7 @@
     total = pl.pallas_call(
         functools.partial(kernel, tm_size, ctx_size),
         out_shape=jax.ShapeDtypeStruct((1, R, D), f32),
-        in_specs=[vmem] * 4 + [hbm] * 3,
+        in_specs=[vmem, vmem, pl.BlockSpec(memory_space=pltpu.SMEM)] + [hbm] * 3,
         out_specs=vmem,
         scratch_shapes=[
             pltpu.VMEM((3, D, half), bf16),
@@ -461,18 +494,18 @@
             dma((2, mid, CHUNKS)), dma((2, mid, CHUNKS)),
             dma, dma,
             dma((ring, CHUNKS)), dma((ring, CHUNKS)),
+            dma((2, 2)), dma((2, 2)),
             dma((2,)), dma((2,)),
-            dma((2,)), dma((2,)),
-            dma((2,)), dma((2,)),
+            dma((2, 2)), dma((2, 2)),
             dma((far,)), dma((far,)),
             dma((far,)), dma((far,)),
-            dma((far,)), dma((far,)),
-            dma((far,)), dma((far,)),
+            dma((far, 2)), dma((far, 2)),
+            dma((far, 2)), dma((far, 2)),
         ],
         compiler_params=pltpu.CompilerParams(
             collective_id=0, has_side_effects=True, vmem_limit_bytes=56 * 1024 * 1024
         ),
-    )(iterate, features, gap, frame_rows, qkv_weight, out_weight, mod_weight)
+    )(iterate, frame_index[None, :], noise_steps, qkv_weight, out_weight, mod_weight)
     return anchor[None] + total
 
 

time: 71.5 us -> 64.7 us (0.905)
  Pallas kernels: 65 us -> 62.2 us
  other arithmetic: 4.9 us -> 2.29 us
  local copies, waits for them, and re-layouts: 1.38 us -> 0.01 us
    pallas_call x1, Pallas kernels: 65 us -> 62.2 us  [per_device(): pl.pallas_call(functools.partial(kernel, tm_size, ctx_size), out_shape=ja...]
    pad x2 -> x0, local copies, waits for them, and re-layouts: 1.26 us -> none  [the longest x1 0.65 us: per_device(): gap = jnp.pad(gap, ((0, Rp - R), (0, 0)))]
    reduce_sum x1 -> x0, other arithmetic: 0.78 us -> none  [token_terms(): jnp.sum(jnp.where(hit, steps_row[None, :], 0), axis=1).astype(jnp.float32)]
    concatenate x2 -> x0, other arithmetic: 0.73 us -> none  [the longest x1 0.65 us: token_terms(): jnp.concatenate([jnp.cos(angles), jnp.sin(angles)], axis=1)]
where the time goes in v3:
time: 64.7 us; the launch traced here: 64.5 us
  Pallas kernels  62.2 us (96%)
  other arithmetic  2.29 us (4%)
    pallas_call x1, Pallas kernels, per_device(): pl.pallas_call(functools.partial(kernel, tm_size, ctx_size), out_shape=ja...  62.2 us
    add x1, other arithmetic, per_device(): return anchor[None] + total  2.29 us

profile of v3, /device:TPU:3, one launch (start us, length us, event | category | flops | bytes accessed | tf_op | source)
XLA Modules:
  0.0 64.5 jit_solution(6096476225518106889)
XLA Ops:
  0.0 0.0 copy-start
  0.0 62.2 %shard_map.73 = f32[1,168,1536]{2,1,0:T(8,128)} custom-call(f32[1,168,1536]{2,1,0:T(8,128)} %latent_ref.1, s32[1,168]{1,0:T(1,128)} %bitcast.3, s32[1,8]{1,0:T(1,128)} %steps_ref.1, bf16[1536,4608]{1,0:T(8,128)(2,1)} %qkv_ref.1, bf16[1536,1536]{1,0:T(8,128)(2,1)} %wo_ref.1, bf16[256,4608]{1,0:T(8,128)(2,1)} %mod_ref.1), custom_call_target="tpu_custom_call" | custom-call | tf_op jit(solution)/shard_map/pallas_call | solution.py:461
  62.2 0.0 copy-done
  62.2 2.3 %bitcast_add_fusion = f32[1,168,1536]{2,1,0:T(8,128)} fusion(f32[1,168,1536]{2,1,0:T(8,128)} %shard_map.73, f32[168,1536]{1,0:T(8,128)S(1)} %copy-done), kind=kLoop, calls=%fused_computation | loop fusion | flops 258048 | bytes 3096576 | tf_op jit(solution)/shard_map/add | solution.py:509
Async XLA Ops:
  0.0 62.2 %copy-start = (f32[168,1536]{1,0:T(8,128)S(1)}, f32[168,1536]{1,0:T(8,128)}, u32[]{:S(2)}) copy-start(f32[168,1536]{1,0:T(8,128)} %param.8) | copy-start | bytes 3096580

commit v4 on v3

--- a/solution.py
+++ b/solution.py
@@ -85,9 +85,9 @@
 
     started = []
 
-    def start(copy):
-        copy.start()
-        started.append(copy)
+    def start(make, *what):
+        make(*what).start()
+        started.append((make, what))
 
     def swap_copy(j):
         return remote(own.at[j], buf.at[0, j, h], swap_send.at[j], swap_recv.at[j], swap_peer)
@@ -169,22 +169,39 @@
                 buf.at[sl, j, 1 - k], buf.at[sl, j, 1 - k], core_send.at[sl, j], core_recv.at[sl, j], core_peer
             ).wait_recv()
 
+    def n_copy(j):
+        return remote(local.at[j], plocal.at[j], n_send.at[j], n_recv.at[j], core_peer)
+
+    def first_steps(record):
+        for j in range(CHUNKS):
+            if not record:
+                swap_landed(j).wait_recv()
+            for make, what in ((ring_copy, (0, 0, j)), (ring_copy, (1, 0, j)), (core_copy, (0, j))):
+                make(*what).start()
+                if record:
+                    started.append((make, what))
+
+    def pass_on(s, record):
+        for j in range(CHUNKS):
+            for way in range(2):
+                ring_copy(way, s - 1, j).wait_recv()
+                sent = [(core_copy, (slot(way, s), j))]
+                if s < mid - 1 or (way == 0 and j == 0) or (way == 1 and j == CHUNKS - 1):
+                    sent.insert(0, (ring_copy, (way, s, j)))
+                if s == mid - 1 and j == 1 and way == 1:
+                    sent.insert(0, (opposite_copy, ()))
+                for make, what in sent:
+                    make(*what).start()
+                    if record:
+                        started.append((make, what))
+
+    @pl.when(k == h)
+    def _():
+        first_steps(True)
+
     for j in range(2):
         local[j] = -gap[:R] * latent_ref[0, :, j * half:(j + 1) * half]
-        start(remote(local.at[j], plocal.at[j], n_send.at[j], n_recv.at[j], core_peer))
-
-    for j in range(CHUNKS):
-        @pl.when(k != h)
-        def _():
-            swap_landed(j).wait_recv()
-
-        for way in range(2):
-            start(ring_copy(way, 0, j))
-        start(core_copy(0, j))
-
-    for j in range(2):
-        gate = jnp.dot(feat, wmod[:, 2 * D + j * half:2 * D + (j + 1) * half], preferred_element_type=jnp.float32)
-        negate[j] = -gap * gate
+        start(n_copy, j)
 
     score_scale = HD ** (-0.5) * math.log2(math.e)
     tiles = half // (2 * HD)
@@ -228,31 +245,82 @@
         key_frame = frames_of(sl)
 
         def tile(j, carry):
-            if sl == 0:
-                qq = project(sl, 0, j)
-                for g in range(2):
-                    qbuf[j, g] = head_norm(qq[:, g * HD:(g + 1) * HD]).reshape(2, Rp, HD)
             keys, values = keys_values(sl, j)
             allowed = key_frame <= qframe[...].reshape(n_rows, 1)
             for g in range(2):
                 part = partial_sums(qbuf[j, g].reshape(n_rows, HD), keys[g], values[g], allowed)
-                part = part.reshape(2, Rp, 2 * HD)
-                if sl == 0:
-                    acc[j, g] = part
-                else:
-                    acc[j, g] += part
+                acc[j, g] += part.reshape(2, Rp, 2 * HD)
             return carry
 
         lax.fori_loop(0, tiles, tile, 0)
 
-    core_wait(0)
+    def project_block(b):
+        def tile(j, carry):
+            cols = pl.ds(pl.multiple_of(j * 2 * HD, 2 * HD), 2 * HD)
+            parts = []
+            for i in range(3):
+                total = None
+                for m in range(CHUNKS):
+                    one = jnp.dot(
+                        buf[0, m, b], wqkv[i, m * wide:(m + 1) * wide, cols], preferred_element_type=jnp.float32
+                    )
+                    total = one if total is None else total + one
+                parts.append(total)
+            ones = jnp.ones((Rp, HD), jnp.bfloat16)
+            for g in range(2):
+                at = slice(g * HD, (g + 1) * HD)
+                qbuf[j, g, b] = head_norm(parts[0][:, at])
+                kbuf[j, g, b] = head_norm(parts[1][:, at])
+                vbuf[j, g, b] = jnp.concatenate([parts[2][:, at].astype(jnp.bfloat16), ones], axis=1)
+            return carry
+
+        lax.fori_loop(0, tiles, tile, 0)
+
+    for i in range(3):
+        loads[1 + i].wait()
+
+    @pl.when(k != h)
+    def _():
+        core_wait(0)
+
+    project_block(h)
+
+    @pl.when(k != h)
+    def _():
+        first_steps(False)
+
+    for j in range(2):
+        gate = jnp.dot(feat, wmod[:, 2 * D + j * half:2 * D + (j + 1) * half], preferred_element_type=jnp.float32)
+        negate[j] = -gap * gate
+
+    @pl.when(k == h)
+    def _():
+        pass_on(1, True)
+        core_wait(0)
+
+    project_block(1 - h)
     diagonal = lax.broadcasted_iota(jnp.int32, (n_rows, n_rows), 0) == lax.broadcasted_iota(
         jnp.int32, (n_rows, n_rows), 1
     )
-    qframe[...] = jnp.sum(jnp.where(diagonal, frames_of(0), 0.0), axis=1, keepdims=True).reshape(2, Rp, 1)
-    for i in range(3):
-        loads[1 + i].wait()
-    attend(0)
+    own_frame = frames_of(0)
+    own_query = jnp.sum(jnp.where(diagonal, own_frame, 0.0), axis=1, keepdims=True)
+    qframe[...] = own_query.reshape(2, Rp, 1)
+
+    def own_tile(j, carry):
+        allowed = own_frame <= qframe[...].reshape(n_rows, 1)
+        for g in range(2):
+            part = partial_sums(
+                qbuf[j, g].reshape(n_rows, HD), kbuf[j, g].reshape(n_rows, HD),
+                vbuf[j, g].reshape(n_rows, 2 * HD), allowed,
+            )
+            acc[j, g] = part.reshape(2, Rp, 2 * HD)
+        return carry
+
+    lax.fori_loop(0, tiles, own_tile, 0)
+
+    @pl.when(k != h)
+    def _():
+        pass_on(1, False)
 
     def later(d):
         return {"tm": 2 * ((a + d) % pairs) + k}
@@ -280,7 +348,7 @@
         )
 
     for j in range(2):
-        remote(local.at[j], plocal.at[j], n_send.at[j], n_recv.at[j], core_peer).wait_recv()
+        n_copy(j).wait_recv()
     xa[...] = local[k] + plocal[k]
     for d in range(1, pairs):
         @pl.when(a + d < pairs)
@@ -291,14 +359,8 @@
         base[j] = jnp.where(k == 1, local[j] + plocal[j], local[j])
 
     for s in range(1, mid):
-        for j in range(CHUNKS):
-            for way in range(2):
-                ring_copy(way, s - 1, j).wait_recv()
-                if s < mid - 1 or (way == 0 and j == 0) or (way == 1 and j == CHUNKS - 1):
-                    start(ring_copy(way, s, j))
-                start(core_copy(slot(way, s), j))
-            if s == mid - 1 and j == 1:
-                start(opposite_copy())
+        if s > 1:
+            pass_on(s, True)
         for way in range(2):
             core_wait(slot(way, s))
             attend(slot(way, s))
@@ -310,18 +372,18 @@
             ya_copy(d).start()
 
     ring_copy(0, mid - 1, 0).wait_recv()
-    start(core_copy(mid, 0))
+    start(core_copy, mid, 0)
     opposite_copy().wait_recv()
-    start(core_copy(mid, 1))
+    start(core_copy, mid, 1)
     ring_copy(1, mid - 1, CHUNKS - 1).wait_recv()
-    start(core_copy(mid, CHUNKS - 1))
+    start(core_copy, mid, CHUNKS - 1)
     core_wait(mid)
 
     def last_tile(j, carry):
         keys, values = keys_values(mid, j)
         for g in range(2):
-            kbuf[j, g] = keys[g]
-            vbuf[j, g] = values[g]
+            kbuf[j, g] = keys[g].reshape(2, Rp, HD)
+            vbuf[j, g] = values[g].reshape(2, Rp, 2 * HD)
         return carry
 
     lax.fori_loop(0, tiles, last_tile, 0)
@@ -332,7 +394,9 @@
         allowed = last_frame <= qframe[b, lo:hi]
         for j in range(tiles):
             for g in range(2):
-                part = partial_sums(qbuf[j, g, b, lo:hi], kbuf[j, g], vbuf[j, g], allowed)
+                part = partial_sums(
+                    qbuf[j, g, b, lo:hi], kbuf[j, g].reshape(n_rows, HD), vbuf[j, g].reshape(n_rows, 2 * HD), allowed
+                )
                 full = acc[j, g, b, lo:hi] + part
                 first = (2 * j + g) * HD
                 atts[m, lo:hi, first:first + HD] = (full[:, :HD] / full[:, HD:]).astype(jnp.bfloat16)
@@ -350,7 +414,7 @@
 
     for i in range(2):
         finish(1 - h, 0, i)
-        start(away(i))
+        start(away, i)
     for i in range(2):
         finish(h, 1, i)
 
@@ -393,7 +457,7 @@
                 )
             drift[j, lo:hi] = negate[j, lo:hi] * branch
             db[j, lo:hi] = drift[j, lo:hi].astype(jnp.bfloat16)
-            start(d_copy(j, i))
+            start(d_copy, j, i)
         for j in range(2):
             d_copy(j, i).wait_recv()
         xs[lo:hi] = (drift[k, lo:hi] + pdb[k, lo:hi].astype(jnp.float32)).astype(jnp.bfloat16)
@@ -420,8 +484,8 @@
     for j in range(2):
         out_ref[0, :, j * half:(j + 1) * half] = base[j]
 
-    for copy in started:
-        copy.wait_send()
+    for make, what in started:
+        make(*what).wait_send()
 
     @pl.when(k != h)
     def _():
@@ -455,7 +519,7 @@
     Rp = (R + 1 + 15) // 16 * 16
     tiles = half // (2 * HD)
     vmem = pl.BlockSpec(memory_space=pltpu.VMEM)
-    hbm = pl.BlockSpec(memory_space=pl.ANY)
+    hbm = pl.BlockSpec(memory_space=pltpu.HBM)
     dma = pltpu.SemaphoreType.DMA
     f32, bf16 = jnp.float32, jnp.bfloat16
     total = pl.pallas_call(
@@ -472,8 +536,8 @@
             pltpu.VMEM((tiles, 2, 2, Rp, HD), bf16),
             pltpu.VMEM((2, Rp, 1), f32),
             pltpu.VMEM((tiles, 2, 2, Rp, 2 * HD), f32),
-            pltpu.VMEM((tiles, 2, 2 * Rp, HD), bf16),
-            pltpu.VMEM((tiles, 2, 2 * Rp, 2 * HD), bf16),
+            pltpu.VMEM((tiles, 2, 2, Rp, HD), bf16),
+            pltpu.VMEM((tiles, 2, 2, Rp, 2 * HD), bf16),
             pltpu.VMEM((2, Rp, half), bf16),
             pltpu.VMEM((2, Rp, half), bf16),
             pltpu.VMEM((2, Rp, half), f32),

time: 64.7 us -> 64.3 us (level)
  no operation moved by 1% of the time
where the time goes in v4:
time: 64.3 us; the launch traced here: 64.1 us
  Pallas kernels  61.8 us (96%)
  other arithmetic  2.29 us (4%)
    pallas_call x1, Pallas kernels, per_device(): pl.pallas_call(functools.partial(kernel, tm_size, ctx_size), out_shape=ja...  61.8 us
    add x1, other arithmetic, per_device(): return anchor[None] + total  2.29 us

profile of v4, /device:TPU:3, one launch (start us, length us, event | category | flops | bytes accessed | tf_op | source)
XLA Modules:
  0.0 64.1 jit_solution(8691752317431856682)
XLA Ops:
  0.0 0.0 copy-start
  0.0 61.8 %shard_map.73 = f32[1,168,1536]{2,1,0:T(8,128)} custom-call(f32[1,168,1536]{2,1,0:T(8,128)} %latent_ref.1, s32[1,168]{1,0:T(1,128)} %bitcast.3, s32[1,8]{1,0:T(1,128)} %steps_ref.1, bf16[1536,4608]{1,0:T(8,128)(2,1)} %qkv_ref.1, bf16[1536,1536]{1,0:T(8,128)(2,1)} %wo_ref.1, bf16[256,4608]{1,0:T(8,128)(2,1)} %mod_ref.1), custom_call_target="tpu_custom_call" | custom-call | tf_op jit(solution)/shard_map/pallas_call | solution.py:525
  61.8 0.0 copy-done
  61.8 2.3 %bitcast_add_fusion = f32[1,168,1536]{2,1,0:T(8,128)} fusion(f32[1,168,1536]{2,1,0:T(8,128)} %shard_map.73, f32[168,1536]{1,0:T(8,128)S(1)} %copy-done), kind=kLoop, calls=%fused_computation | loop fusion | flops 258048 | bytes 3096576 | tf_op jit(solution)/shard_map/add | solution.py:573
Async XLA Ops:
  0.0 61.8 %copy-start = (f32[168,1536]{1,0:T(8,128)S(1)}, f32[168,1536]{1,0:T(8,128)}, u32[]{:S(2)}) copy-start(f32[168,1536]{1,0:T(8,128)} %param.8) | copy-start | bytes 3096580

commit v5 on v4

--- a/solution.py
+++ b/solution.py
@@ -135,9 +135,10 @@
         if j == 0:
             pl.semaphore_wait(barrier, len(greeted))
 
-        @pl.when(k != h)
-        def _():
-            swap_copy(j).start()
+        if j == 0:
+            @pl.when(k != h)
+            def _():
+                swap_copy(0).start()
 
         @pl.when(k == h)
         def _():
@@ -172,14 +173,20 @@
     def n_copy(j):
         return remote(local.at[j], plocal.at[j], n_send.at[j], n_recv.at[j], core_peer)
 
-    def first_steps(record):
+    def ring_step(j, record):
+        for way in range(2):
+            ring_copy(way, 0, j).start()
+            if record:
+                started.append((ring_copy, (way, 0, j)))
+
+    def swapped_steps():
         for j in range(CHUNKS):
-            if not record:
-                swap_landed(j).wait_recv()
-            for make, what in ((ring_copy, (0, 0, j)), (ring_copy, (1, 0, j)), (core_copy, (0, j))):
-                make(*what).start()
-                if record:
-                    started.append((make, what))
+            if j + 1 < CHUNKS:
+                swap_copy(j).wait_send()
+                swap_copy(j + 1).start()
+            swap_landed(j).wait_recv()
+            ring_step(j, False)
+            core_copy(0, j).start()
 
     def pass_on(s, record):
         for j in range(CHUNKS):
@@ -197,7 +204,10 @@
 
     @pl.when(k == h)
     def _():
-        first_steps(True)
+        ring_step(0, True)
+        for j in range(CHUNKS):
+            core_copy(0, j).start()
+            started.append((core_copy, (0, j)))
 
     for j in range(2):
         local[j] = -gap[:R] * latent_ref[0, :, j * half:(j + 1) * half]
@@ -281,13 +291,15 @@
 
     @pl.when(k != h)
     def _():
+        swapped_steps()
         core_wait(0)
 
     project_block(h)
 
-    @pl.when(k != h)
-    def _():
-        first_steps(False)
+    @pl.when(k == h)
+    def _():
+        for j in range(1, CHUNKS):
+            ring_step(j, True)
 
     for j in range(2):
         gate = jnp.dot(feat, wmod[:, 2 * D + j * half:2 * D + (j + 1) * half], preferred_element_type=jnp.float32)
@@ -414,13 +426,17 @@
 
     for i in range(2):
         finish(1 - h, 0, i)
-        start(away, i)
+        if i == 0:
+            away(0).start()
     for i in range(2):
         finish(h, 1, i)
 
         @pl.when(k != h)
         def _():
             across(i).start()
+
+    away(0).wait_send()
+    start(away, 1)
 
     @pl.when(k == h)
     def _():
@@ -489,8 +505,7 @@
 
     @pl.when(k != h)
     def _():
-        for j in range(CHUNKS):
-            swap_copy(j).wait_send()
+        swap_copy(CHUNKS - 1).wait_send()
         for i in range(2):
             across(i).wait_send()
 

time: 64.3 us -> 66.1 us (1.028)
  Pallas kernels: 61.8 us -> 62.9 us
    pallas_call x1, Pallas kernels: 61.8 us -> 62.9 us  [per_device(): pl.pallas_call(functools.partial(kernel, tm_size, ctx_size), out_shape=ja...]
where the time goes in v5:
time: 66.1 us; the launch traced here: 65.2 us
  Pallas kernels  62.9 us (95%)
  other arithmetic  2.29 us (3%)
    pallas_call x1, Pallas kernels, per_device(): pl.pallas_call(functools.partial(kernel, tm_size, ctx_size), out_shape=ja...  62.9 us
    add x1, other arithmetic, per_device(): return anchor[None] + total  2.29 us

profile of v5, /device:TPU:3, one launch (start us, length us, event | category | flops | bytes accessed | tf_op | source)
XLA Modules:
  0.0 65.2 jit_solution(2901135191759105044)
XLA Ops:
  0.0 0.0 copy-start
  0.0 62.9 %shard_map.73 = f32[1,168,1536]{2,1,0:T(8,128)} custom-call(f32[1,168,1536]{2,1,0:T(8,128)} %latent_ref.1, s32[1,168]{1,0:T(1,128)} %bitcast.3, s32[1,8]{1,0:T(1,128)} %steps_ref.1, bf16[1536,4608]{1,0:T(8,128)(2,1)} %qkv_ref.1, bf16[1536,1536]{1,0:T(8,128)(2,1)} %wo_ref.1, bf16[256,4608]{1,0:T(8,128)(2,1)} %mod_ref.1), custom_call_target="tpu_custom_call" | custom-call | tf_op jit(solution)/shard_map/pallas_call | solution.py:540
  62.9 0.0 copy-done
  62.9 2.3 %bitcast_add_fusion = f32[1,168,1536]{2,1,0:T(8,128)} fusion(f32[1,168,1536]{2,1,0:T(8,128)} %shard_map.73, f32[168,1536]{1,0:T(8,128)S(1)} %copy-done), kind=kLoop, calls=%fused_computation | loop fusion | flops 258048 | bytes 3096576 | tf_op jit(solution)/shard_map/add | solution.py:588
Async XLA Ops:
  0.0 62.9 %copy-start = (f32[168,1536]{1,0:T(8,128)S(1)}, f32[168,1536]{1,0:T(8,128)}, u32[]{:S(2)}) copy-start(f32[168,1536]{1,0:T(8,128)} %param.8) | copy-start | bytes 3096580

commit v6 on v4

--- a/solution.py
+++ b/solution.py
@@ -281,13 +281,10 @@
 
     @pl.when(k != h)
     def _():
+        first_steps(False)
         core_wait(0)
 
     project_block(h)
-
-    @pl.when(k != h)
-    def _():
-        first_steps(False)
 
     for j in range(2):
         gate = jnp.dot(feat, wmod[:, 2 * D + j * half:2 * D + (j + 1) * half], preferred_element_type=jnp.float32)

time: 64.3 us -> 65 us (1.011)
    pallas_call x1, Pallas kernels: 61.8 us -> 62.4 us  [per_device(): pl.pallas_call(functools.partial(kernel, tm_size, ctx_size), out_shape=ja...]
where the time goes in v6:
time: 65 us; the launch traced here: 64.8 us
  Pallas kernels  62.4 us (96%)
  other arithmetic  2.29 us (4%)
    pallas_call x1, Pallas kernels, per_device(): pl.pallas_call(functools.partial(kernel, tm_size, ctx_size), out_shape=ja...  62.4 us
    add x1, other arithmetic, per_device(): return anchor[None] + total  2.29 us

profile of v6, /device:TPU:3, one launch (start us, length us, event | category | flops | bytes accessed | tf_op | source)
XLA Modules:
  0.0 64.8 jit_solution(14247168415586382208)
XLA Ops:
  0.0 0.0 copy-start
  0.0 62.4 %shard_map.73 = f32[1,168,1536]{2,1,0:T(8,128)} custom-call(f32[1,168,1536]{2,1,0:T(8,128)} %latent_ref.1, s32[1,168]{1,0:T(1,128)} %bitcast.3, s32[1,8]{1,0:T(1,128)} %steps_ref.1, bf16[1536,4608]{1,0:T(8,128)(2,1)} %qkv_ref.1, bf16[1536,1536]{1,0:T(8,128)(2,1)} %wo_ref.1, bf16[256,4608]{1,0:T(8,128)(2,1)} %mod_ref.1), custom_call_target="tpu_custom_call" | custom-call | tf_op jit(solution)/shard_map/pallas_call | solution.py:522
  62.4 0.0 copy-done
  62.5 2.3 %bitcast_add_fusion = f32[1,168,1536]{2,1,0:T(8,128)} fusion(f32[1,168,1536]{2,1,0:T(8,128)} %shard_map.73, f32[168,1536]{1,0:T(8,128)S(1)} %copy-done), kind=kLoop, calls=%fused_computation | loop fusion | flops 258048 | bytes 3096576 | tf_op jit(solution)/shard_map/add | solution.py:570
Async XLA Ops:
  0.0 62.5 %copy-start = (f32[168,1536]{1,0:T(8,128)S(1)}, f32[168,1536]{1,0:T(8,128)}, u32[]{:S(2)}) copy-start(f32[168,1536]{1,0:T(8,128)} %param.8) | copy-start | bytes 3096580
